TPU v7x, 32 devices: a whole 2x2x4 slice. The times are simulated.
32 devices in a mesh: dp: 8 (over z, x), shard: 4 (over y, core).
Axes of the slice: x: 2, y: 2, z: 4, core: 2. Of those that a mesh axis runs over, the one named last changes fastest.
Arguments:
- patches: bfloat16 [64, 1024, 384], P(('dp', 'shard')), may hold values from -6 to 6
- segments: int32 [64, 1024], P(('dp', 'shard')), may hold values from 0 to 7, never falling along the last dimension, each value on 1 to 256 neighbouring positions
- out_grad: bfloat16 [64, 1024, 384], P(('dp', 'shard')), may hold values from -6 to 6
- master: float32 [1775104], P('shard'), may hold values from -6 to 6
- moment_one: float32 [1775104], P('shard'), may hold values from -6 to 6
- moment_two: float32 [1775104], P('shard'), may hold values from 0.1 to 10
Outputs:
- activations: bfloat16 [64, 1024, 384], P(('dp', 'shard'))
- input_grad: bfloat16 [64, 1024, 384], P(('dp', 'shard'))
- grad_sum: float32 [1775104], P('shard')
- vector_grad: float32 [5632], replicated
- new_master: float32 [1775104], P('shard')
- new_moment_one: float32 [1775104], P('shard')
- new_moment_two: float32 [1775104], P('shard')
- weights_copy: bfloat16 [1775104], replicated
All inputs are finite; a program needn't handle non-finite values.
Results may differ from a plain program's by a relative error of at most 0.015.
Values may be sent and summed in bfloat16 or wider, within the bound.
A program may use at most 192 MiB of HBM per device.

v0:
```python
from functools import partial
import math

import jax
import jax.numpy as jnp
from jax import lax
from jax.sharding import PartitionSpec as P

D = 384
HEADS = 6
HD = 64
FF = 1536
STEP = 3
PARAMS = 1775104


NORM_EPS = 1e-06
MASKED = -1e30
BETA_ONE = 0.5
BETA_TWO = 0.5
RATE = 0.03
DECAY = 0.1
ADAM_EPS = 1e-08


def layout():
    return [
        ("qkv_weight", (D, 3 * D)),
        ("out_weight", (D, D)),
        ("up_weight", (D, FF)),
        ("down_weight", (FF, D)),
        ("norm_gain", (D,)),
        ("norm_bias", (D,)),
        ("qkv_bias", (3 * D,)),
        ("query_gain", (HD,)),
        ("query_bias", (HD,)),
        ("key_gain", (HD,)),
        ("key_bias", (HD,)),
        ("out_bias", (D,)),
        ("mlp_gain", (D,)),
        ("mlp_bias", (D,)),
        ("up_bias", (FF,)),
        ("down_bias", (D,)),
    ]


def unpack(flat_vec):
    params = {}
    offset = 0
    for entry_name, entry_shape in layout():
        entry_count = math.prod(entry_shape)
        params[entry_name] = flat_vec[offset : offset + entry_count].reshape(entry_shape)
        offset = offset + entry_count
    return params


def layer_norm(inputs, gain_vec, bias_vec):
    average = jnp.mean(inputs, axis=-1, keepdims=True)
    centered = inputs - average
    variance = jnp.mean(centered * centered, axis=-1, keepdims=True)
    return centered * lax.rsqrt(variance + NORM_EPS) * gain_vec + bias_vec


def gelu_exact(values_in):
    return jax.nn.gelu(values_in, approximate=False)


def masked_scores(queries, block_ids, key_rows, segment_ids):
    score_scale = queries.shape[-1] ** (-0.5)
    scores = (
        jnp.einsum("qhd,khd->hqk", queries, key_rows, preferred_element_type=jnp.float32)
        * score_scale
    )
    same_image = block_ids[:, None] == segment_ids[None, :]
    return jnp.where(same_image[None], scores, MASKED)


def forward_block(block_item, key_rows, value_rows, segment_ids):
    queries, block_ids = block_item
    scores = masked_scores(queries, block_ids, key_rows, segment_ids)
    row_peak = jnp.max(scores, axis=-1, keepdims=True)
    exponent = jnp.exp(scores - row_peak)
    totals = jnp.sum(exponent, axis=-1, keepdims=True)
    attn_probs = (exponent / totals).astype(jnp.bfloat16)
    attended = jnp.einsum(
        "hqk,khd->qhd", attn_probs, value_rows, preferred_element_type=jnp.float32
    )
    return (attended, row_peak + jnp.log(totals))


def backward_block(grads_carry, block_item, key_rows, value_rows, segment_ids):
    key_grad, value_grad = grads_carry
    queries, block_ids, log_norm, mixed_grad = block_item
    score_scale = queries.shape[-1] ** (-0.5)
    scores = masked_scores(queries, block_ids, key_rows, segment_ids)
    attn_probs = jnp.exp(scores - log_norm)
    value_grad = value_grad + jnp.einsum(
        "hqk,qhd->khd",
        attn_probs.astype(jnp.bfloat16),
        mixed_grad,
        preferred_element_type=jnp.float32,
    )
    probs_grad = jnp.einsum(
        "qhd,khd->hqk", mixed_grad, value_rows, preferred_element_type=jnp.float32
    )
    inner_sum = jnp.sum(attn_probs * probs_grad, axis=-1, keepdims=True)
    score_grad = (attn_probs * (probs_grad - inner_sum)).astype(jnp.bfloat16)
    query_grad = (
        jnp.einsum("hqk,khd->qhd", score_grad, key_rows, preferred_element_type=jnp.float32)
        * score_scale
    )
    key_grad = (
        key_grad
        + jnp.einsum("hqk,qhd->khd", score_grad, queries, preferred_element_type=jnp.float32)
        * score_scale
    )
    return ((key_grad, value_grad), query_grad)


def layer_pass(inputs, segment_ids, cotangent, params):
    row_count, width = inputs.shape
    small = {
        entry_name: params[entry_name].astype(jnp.float32)
        for entry_name, entry_shape in layout()
        if len(entry_shape) == 1
    }
    inputs_f = inputs.astype(jnp.float32)
    normed_in, first_pull = jax.vjp(layer_norm, inputs_f, small["norm_gain"], small["norm_bias"])
    normed_low = normed_in.astype(jnp.bfloat16)
    projected = (
        jnp.dot(normed_low, params["qkv_weight"], preferred_element_type=jnp.float32)
        + small["qkv_bias"]
    )
    split_cols = projected.reshape(row_count, 3, HEADS, HD)
    query_normed, query_pull = jax.vjp(
        layer_norm, split_cols[:, 0], small["query_gain"], small["query_bias"]
    )
    key_normed, key_pull = jax.vjp(
        layer_norm, split_cols[:, 1], small["key_gain"], small["key_bias"]
    )
    queries = query_normed.astype(jnp.bfloat16)
    key_rows = key_normed.astype(jnp.bfloat16)
    value_rows = split_cols[:, 2].astype(jnp.bfloat16)
    block_rows = min(512, row_count)
    count_blocks = row_count // block_rows
    query_blocks = queries.reshape(count_blocks, block_rows, HEADS, HD)
    id_blocks = segment_ids.reshape(count_blocks, block_rows)
    attended, log_norm = lax.map(
        partial(forward_block, key_rows=key_rows, value_rows=value_rows, segment_ids=segment_ids),
        (query_blocks, id_blocks),
    )
    mixed_low = attended.reshape(row_count, width).astype(jnp.bfloat16)
    residual = (
        inputs_f
        + jnp.dot(mixed_low, params["out_weight"], preferred_element_type=jnp.float32)
        + small["out_bias"]
    )
    normed_mid, second_pull = jax.vjp(layer_norm, residual, small["mlp_gain"], small["mlp_bias"])
    mid_low = normed_mid.astype(jnp.bfloat16)
    hidden_pre = (
        jnp.dot(mid_low, params["up_weight"], preferred_element_type=jnp.float32) + small["up_bias"]
    )
    hidden_act, gelu_pull = jax.vjp(gelu_exact, hidden_pre)
    hidden_low = hidden_act.astype(jnp.bfloat16)
    output = (
        residual
        + jnp.dot(hidden_low, params["down_weight"], preferred_element_type=jnp.float32)
        + small["down_bias"]
    ).astype(jnp.bfloat16)
    cot_f = cotangent.astype(jnp.float32)
    grad_down = jnp.einsum("sf,sd->fd", hidden_low, cotangent, preferred_element_type=jnp.float32)
    grad_down_bias = jnp.sum(cot_f, axis=0)
    act_grad = jnp.einsum(
        "sd,fd->sf", cotangent, params["down_weight"], preferred_element_type=jnp.float32
    )
    pre_grad = gelu_pull(act_grad)[0].astype(jnp.bfloat16)
    grad_up = jnp.einsum("sd,sf->df", mid_low, pre_grad, preferred_element_type=jnp.float32)
    grad_up_bias = jnp.sum(pre_grad.astype(jnp.float32), axis=0)
    mid_grad = jnp.einsum(
        "sf,df->sd", pre_grad, params["up_weight"], preferred_element_type=jnp.float32
    )
    resid_back, grad_mlp_gain, grad_mlp_bias = second_pull(mid_grad)
    resid_grad = cot_f + resid_back
    branch_grad = resid_grad.astype(jnp.bfloat16)
    grad_out = jnp.einsum("sc,sd->cd", mixed_low, branch_grad, preferred_element_type=jnp.float32)
    grad_out_bias = jnp.sum(branch_grad.astype(jnp.float32), axis=0)
    mixed_grad = jnp.einsum(
        "sd,cd->sc", branch_grad, params["out_weight"], preferred_element_type=jnp.float32
    )
    mixed_grad = mixed_grad.astype(jnp.bfloat16).reshape(count_blocks, block_rows, HEADS, HD)
    zero_rows = jnp.zeros((row_count, HEADS, HD), jnp.float32)
    (key_grad, value_grad), query_grad = lax.scan(
        partial(backward_block, key_rows=key_rows, value_rows=value_rows, segment_ids=segment_ids),
        (zero_rows, zero_rows),
        (query_blocks, id_blocks, log_norm, mixed_grad),
    )
    query_grad = query_grad.reshape(row_count, HEADS, HD)
    raw_query_grad, grad_query_gain, grad_query_bias = query_pull(query_grad)
    raw_key_grad, grad_key_gain, grad_key_bias = key_pull(key_grad)
    proj_grad = jnp.stack([raw_query_grad, raw_key_grad, value_grad], axis=1)
    proj_grad = proj_grad.reshape(row_count, 3 * width).astype(jnp.bfloat16)
    grad_qkv = jnp.einsum("sc,sd->cd", normed_low, proj_grad, preferred_element_type=jnp.float32)
    grad_qkv_bias = jnp.sum(proj_grad.astype(jnp.float32), axis=0)
    in_grad = jnp.einsum(
        "sd,cd->sc", proj_grad, params["qkv_weight"], preferred_element_type=jnp.float32
    )
    input_back, grad_norm_gain, grad_norm_bias = first_pull(in_grad)
    input_grad = (resid_grad + input_back).astype(jnp.bfloat16)
    pieces = [
        grad_qkv,
        grad_out,
        grad_up,
        grad_down,
        grad_norm_gain,
        grad_norm_bias,
        grad_qkv_bias,
        grad_query_gain,
        grad_query_bias,
        grad_key_gain,
        grad_key_bias,
        grad_out_bias,
        grad_mlp_gain,
        grad_mlp_bias,
        grad_up_bias,
        grad_down_bias,
    ]
    pieces = [piece_grad.reshape(-1) for piece_grad in pieces]
    used_count = sum((piece_grad.shape[0] for piece_grad in pieces))
    pieces.append(jnp.zeros((PARAMS - used_count,), jnp.float32))
    return (output, input_grad, jnp.concatenate(pieces))


def shards(patches, segments, out_grad, master, moment_one, moment_two):
    weights = lax.all_gather(master.astype(jnp.bfloat16), "shard", axis=0, tiled=True)
    params = unpack(weights)

    def per_sequence(running, sequence_item):
        inputs, segment_ids, cotangent = sequence_item
        output, input_grad, flat_grad = layer_pass(inputs, segment_ids, cotangent, params)
        return (running + flat_grad, (output, input_grad))

    running, (activations, input_grad) = lax.scan(
        per_sequence, jnp.zeros((weights.shape[0],), jnp.float32), (patches, segments, out_grad)
    )
    sequences = patches.shape[0] * lax.axis_size("dp") * lax.axis_size("shard")
    matrix_count = 4 * D * D + 2 * D * FF
    vector_sum = lax.psum(running[matrix_count:], ("dp", "shard"))
    vector_grad = vector_sum / sequences
    owned_sum = lax.psum_scatter(
        running.astype(jnp.bfloat16), "shard", scatter_dimension=0, tiled=True
    ).astype(jnp.float32)
    owned_sum = lax.psum(owned_sum, "dp")
    grad_sum = owned_sum / sequences
    first_moment = BETA_ONE * moment_one + (1.0 - BETA_ONE) * grad_sum
    second_moment = BETA_TWO * moment_two + (1.0 - BETA_TWO) * grad_sum * grad_sum
    first_hat = first_moment / (1.0 - BETA_ONE**STEP)
    second_hat = second_moment / (1.0 - BETA_TWO**STEP)
    quarter = grad_sum.shape[0]
    positions = lax.axis_index("shard") * quarter + jnp.arange(quarter, dtype=jnp.int32)
    matrix_mask = (positions < matrix_count).astype(jnp.float32)
    new_master = master - RATE * (
        first_hat / (jnp.sqrt(second_hat) + ADAM_EPS) + DECAY * matrix_mask * master
    )
    weights_copy = lax.all_gather(new_master.astype(jnp.bfloat16), "shard", axis=0, tiled=True)
    return (
        activations,
        input_grad,
        grad_sum,
        vector_grad,
        new_master,
        first_moment,
        second_moment,
        weights_copy,
    )


def solution(mesh):
    placed = (
        P(("dp", "shard"), None, None),
        P(("dp", "shard"), None),
        P(("dp", "shard"), None, None),
        P("shard"),
        P("shard"),
        P("shard"),
    )
    return jax.shard_map(
        shards,
        mesh=mesh,
        in_specs=placed,
        out_specs=(
            P(("dp", "shard"), None, None),
            P(("dp", "shard"), None, None),
            P("shard"),
            P(),
            P("shard"),
            P("shard"),
            P("shard"),
            P(),
        ),
        check_vma=False,
    )
```

profile of v0, /device:TPU:0, one launch (start us, length us, event | category | flops | bytes accessed | tf_op | source)
XLA Modules:
  0.0 1040.0 jit_solution(10415763913104213330)
XLA Ops:
  8.8 10.9 %reshape.384 = bf16[1,1,443776]{2,1,0:T(2,128)(2,1)} reshape(bf16[443776]{0:T(1024)(128)(2,1)S(1)} %convert_element_type.186) | data formatting | bytes 1775104
  19.9 53.6 %all-gather.5.cloned.1.call-done = bf16[4,1,443776]{2,1,0:T(2,128)(2,1)} async-done(((bf16[1,1,443776]{2,1,0:T(2,128)(2,1)}), bf16[4,1,443776]{2,1,0:T(2,128)(2,1)}) %all-gather.5.cloned.1.call-update) | async-done | bytes 3550224 | tf_op jit(solution)/shard_map/all_gather | solution.py:234
  73.5 64.1 %reduce.8 = bf16[4,443776]{1,0:T(4,128)(2,1)} reduce(bf16[4,1,443776]{2,1,0:T(2,128)(2,1)} %all-gather.5.cloned.1.call-done, bf16[]{:T(256)} %constant.189), dimensions={1}, to_apply=%all-gather.reduce_sub_computation | reduce | bytes 7100418 | tf_op jit(solution)/shard_map/all_gather | solution.py:234
  156.5 562.1 %while.51 = (s32[]{:T(128)}, f32[1775104]{0:T(1024)}, bf16[2,1024,384]{2,1,0:T(8,128)(2,1)}, bf16[2,1024,384]{2,1,0:T(8,128)(2,1)}, bf16[2,1024,384]{2,1,0:T(8,1...) while((s32[]{:T(128)}, f32[1775104]{0:T(1024)}, ...), condition=%wide.region_36.37_spmd.clone.clone, body=%wide.region_0.36_spmd.clone.sunk.clone | while | flops 13979810816 | bytes 577248512 | solution.py:242
  173.1 6.5 copy.110
  192.9 23.7 %while.49 = (s32[]{:T(128)}, bf16[2,512,6,64]{1,3,2,0:T(8,128)(2,1)}, f32[2,6,512,1]{2,1,3,0:T(8,128)S(1)}, s32[2,512]{1,0:T(2,128)S(1)}, s32[1024]{0:T(1024)S(1...) while((s32[]{:T(128)}, ...), condition=%wide.region_10.10_spmd, body=%wide.region_7.9_spmd.sunk | while | flops 843576320 | bytes 49019052 | solution.py:148
  220.6 15.5 %multiply_convert_fusion.6 = (bf16[1024,1536]{1,0:T(8,128)(2,1)S(1)}, f32[1024,1536]{1,0:T(8,128)S(1)}, f32[1024,1536]{1,0:T(8,128)S(1)}) fusion(f32[1536]{0:T(1024)S(1)} %copy-done.67, bf16[384,1536]{1,0:T(8,128)(2,1)S(1)} %copy-done.54, f32[1024,384]{0,1:T(8,128)S(1)} %get-tuple-element.1077, f32[384]{0:T(512)S(1)} %copy-done.78, ...), kind=kOutput, calls=%fused_computation.51.clone.1.clone | convolution fusion | flops 1313734656 | bytes 18498560 | tf_op jit(solution)/shard_map/while/body/eval_jaxpr/dot_general | solution.py:161
  279.4 49.3 %while.50 = (s32[]{:T(128)}, f32[1024,6,64]{0,2,1:T(8,128)S(1)}, f32[1024,6,64]{0,2,1:T(8,128)}, f32[2,512,6,64]{1,3,2,0:T(8,128)}, bf16[2,512,6,64]{1,3,2,0:T(8...) while((s32[]{:T(128)}, f32[1024,6,64]{0,2,1:T(8,128)S(1)}, ...), condition=%wide.region_17.17_spmd.clone, body=%wide.region_15.16_spmd.clone.sunk | while | flops 2063135744 | bytes 139041104 | solution.py:192
  285.4 7.2 multiply_reduce_fusion.21
  292.6 6.9 multiply_convert_fusion.5
  309.9 7.2 multiply_reduce_fusion.21
  317.1 6.9 multiply_convert_fusion.5
  336.2 6.5 multiply_reduce_fusion.26
  361.1 64.6 %concatenate.6 = f32[1775104]{0:T(1024)} concatenate(f32[442368]{0:T(1024)} %reshape.426, f32[147456]{0:T(1024)} %reshape.427, f32[589824]{0:T(1024)} %reshape.428, f32[589824]{0:T(1024)} %reshape.429, f32[384]{0:T(512)S(1)} %get-tuple-element.1100, f32[384]{0:T(512)S(1)} %get-tuple-element.1101, f32[1152]{0:T(1024)S(1)} %reduce_sum.463, f32[64]{0:T(128)S(1)} %get-tuple-element.1103, ...), dimensions={0} | concatenate | bytes 14200832 | tf_op jit(solution)/shard_map/while/body/eval_jaxpr/concatenate | solution.py:230
  450.3 6.2 copy.110
  469.9 23.9 %while.49 = (s32[]{:T(128)}, bf16[2,512,6,64]{1,3,2,0:T(8,128)(2,1)}, f32[2,6,512,1]{2,1,3,0:T(8,128)S(1)}, s32[2,512]{1,0:T(2,128)S(1)}, s32[1024]{0:T(1024)S(1...) while((s32[]{:T(128)}, ...), condition=%wide.region_10.10_spmd, body=%wide.region_7.9_spmd.sunk | while | flops 843576320 | bytes 49019052 | solution.py:148
  497.9 15.3 %multiply_convert_fusion.6 = (bf16[1024,1536]{1,0:T(8,128)(2,1)S(1)}, f32[1024,1536]{1,0:T(8,128)S(1)}, f32[1024,1536]{1,0:T(8,128)S(1)}) fusion(f32[1536]{0:T(1024)S(1)} %copy-done.67, bf16[384,1536]{1,0:T(8,128)(2,1)S(1)} %copy-done.54, f32[1024,384]{0,1:T(8,128)S(1)} %get-tuple-element.1077, f32[384]{0:T(512)S(1)} %copy-done.78, ...), kind=kOutput, calls=%fused_computation.51.clone.1.clone | convolution fusion | flops 1313734656 | bytes 18498560 | tf_op jit(solution)/shard_map/while/body/eval_jaxpr/dot_general | solution.py:161
  556.4 49.5 %while.50 = (s32[]{:T(128)}, f32[1024,6,64]{0,2,1:T(8,128)S(1)}, f32[1024,6,64]{0,2,1:T(8,128)}, f32[2,512,6,64]{1,3,2,0:T(8,128)}, bf16[2,512,6,64]{1,3,2,0:T(8...) while((s32[]{:T(128)}, f32[1024,6,64]{0,2,1:T(8,128)S(1)}, ...), condition=%wide.region_17.17_spmd.clone, body=%wide.region_15.16_spmd.clone.sunk | while | flops 2063135744 | bytes 139041104 | solution.py:192
  562.7 7.2 multiply_reduce_fusion.21
  569.9 6.9 multiply_convert_fusion.5
  587.1 7.2 multiply_reduce_fusion.21
  594.4 6.9 multiply_convert_fusion.5
  613.4 6.5 multiply_reduce_fusion.26
  638.2 64.6 %concatenate.6 = f32[1775104]{0:T(1024)} concatenate(f32[442368]{0:T(1024)} %reshape.426, f32[147456]{0:T(1024)} %reshape.427, f32[589824]{0:T(1024)} %reshape.428, f32[589824]{0:T(1024)} %reshape.429, f32[384]{0:T(512)S(1)} %get-tuple-element.1100, f32[384]{0:T(512)S(1)} %get-tuple-element.1101, f32[1152]{0:T(1024)S(1)} %reduce_sum.463, f32[64]{0:T(128)S(1)} %get-tuple-element.1103, ...), dimensions={0} | concatenate | bytes 14200832 | tf_op jit(solution)/shard_map/while/body/eval_jaxpr/concatenate | solution.py:230
  702.9 8.5 select_add_fusion.3
  725.0 73.5 %all-reduce.6.cloned.1.call-done = bf16[1775104]{0:T(1024)(128)(2,1)} async-done(((bf16[1775104]{0:T(1024)(128)(2,1)}), bf16[1775104]{0:T(1024)(128)(2,1)}) %all-reduce.6.cloned.1.call-update) | async-done | bytes 3550224
  801.5 96.4 %all-reduce.4.cloned.1.call-done = f32[443776]{0:T(1024)} async-done(((f32[443776]{0:T(1024)}), f32[443776]{0:T(1024)}) %all-reduce.4.cloned.1.call-update) | async-done | bytes 1775120 | tf_op jit(solution)/shard_map/psum | solution.py:252
  897.9 6.2 fusion.93
  904.1 10.8 %reshape.386 = bf16[1,1,443776]{2,1,0:T(2,128)(2,1)} reshape(bf16[443776]{0:T(1024)(128)(2,1)S(1)} %get-tuple-element.608) | data formatting | bytes 1775104
  915.7 40.9 %psum.15 = f32[5632]{0:T(1024)S(1)} all-reduce(f32[5632]{0:T(1024)S(1)} %slice.77), channel_id=1, replica_groups=mesh['dp'=8,'shard'=4] {'dp','shard'}, use_global_device_ids=true, to_apply=%region_39.40 | all-reduce | flops 5632 | bytes 45056 | tf_op jit(solution)/shard_map/psum | solution.py:247
  957.3 9.3 all-gather.7.cloned.1.call-done
  966.6 62.3 %reduce.9 = bf16[4,443776]{1,0:T(4,128)(2,1)S(1)} reduce(bf16[4,1,443776]{2,1,0:T(2,128)(2,1)} %all-gather.7.cloned.1.call-done, bf16[]{:T(256)} %constant.189), dimensions={1}, to_apply=%all-gather.1.reduce_sub_computation | reduce | bytes 7100418 | tf_op jit(solution)/shard_map/all_gather | solution.py:264
  (695 shorter events, 336.7 us)
Async XLA Ops:
  7.2 66.4 %all-gather.5.cloned.1.call-start = ((), (), s32[]{:S(2)}) async-start(), calls=%async_computation.1 | async-start | bytes 8875520 | tf_op jit(solution)/shard_map/all_gather | solution.py:234
  19.7 778.9 %all-reduce.6.cloned.1.call-start = ((), (), s32[]{:S(2)}) async-start(), calls=%async_computation.3 | async-start | bytes 7102464
  156.7 115.3 %copy-start.29 = (bf16[384,384]{1,0:T(8,128)(2,1)}, bf16[384,384]{1,0:T(8,128)(2,1)S(1)}, u32[]{:S(2)}) copy-start(bf16[384,384]{1,0:T(8,128)(2,1)S(1)} %get-tuple-element.1282) | copy-start | bytes 884740 | tf_op jit(solution)/shard_map/while
  156.8 31.6 %copy-start.64 = (f32[64]{0:T(128)}, f32[64]{0:T(128)S(1)}, u32[]{:S(2)}) copy-start(f32[64]{0:T(128)S(1)} %convert_element_type.425) | copy-start | bytes 772 | tf_op jit(solution)/shard_map/while
  158.5 9.6 copy-start.61
  159.1 9.0 copy-start.76
  166.7 52.3 %copy-start.2 = (bf16[1,1024,384]{1,2,0:T(8,128)(2,1)}, bf16[1,1024,384]{1,2,0:T(8,128)(2,1)S(1)}, u32[]{:S(2)}) copy-start(bf16[1,1024,384]{1,2,0:T(8,128)(2,1)S(1)} %copy.109) | copy-start | bytes 2359300 | tf_op jit(solution)/shard_map/while
  166.9 6.2 copy-start.50
  219.8 21.8 %copy-start.6 = (f32[1024,384]{0,1:T(8,128)}, f32[1024,384]{0,1:T(8,128)S(1)}, u32[]{:S(2)}) copy-start(f32[1024,384]{0,1:T(8,128)S(1)} %get-tuple-element.1077) | copy-start | bytes 4718596 | tf_op jit(solution)/shard_map/while
  220.6 15.5 %copy-start.22 = (bf16[1,1024,384]{2,1,0:T(8,128)(2,1)S(1)}, bf16[1,1024,384]{2,1,0:T(8,128)(2,1)}, u32[]{:S(2)}) copy-start(bf16[1,1024,384]{2,1,0:T(8,128)(2,1)} %copy-done.21) | copy-start | bytes 2359300 | tf_op jit(solution)/shard_map/while
  220.6 15.5 %copy-start.53 = (bf16[1536,384]{1,0:T(8,128)(2,1)S(1)}, bf16[1536,384]{1,0:T(8,128)(2,1)}, u32[]{:S(2)}) copy-start(bf16[1536,384]{1,0:T(8,128)(2,1)} %get-tuple-element.1288) | copy-start | bytes 3538948 | tf_op jit(solution)/shard_map/while
  279.4 51.1 %copy-start.32 = (f32[1024,6]{0,1:T(8,128)S(1)}, f32[1024,6]{0,1:T(8,128)}, u32[]{:S(2)}) copy-start(f32[1024,6]{0,1:T(8,128)} %copy-done.31) | copy-start | bytes 73732 | tf_op jit(solution)/shard_map/while
  279.4 51.2 %copy-start.65 = (f32[64]{0:T(128)S(1)}, f32[64]{0:T(128)}, u32[]{:S(2)}) copy-start(f32[64]{0:T(128)} %copy-done.64) | copy-start | bytes 772 | tf_op jit(solution)/shard_map/while
  285.4 7.2 copy-start.27
  309.9 7.2 copy-start.27
  434.0 115.0 %copy-start.29 = (bf16[384,384]{1,0:T(8,128)(2,1)}, bf16[384,384]{1,0:T(8,128)(2,1)S(1)}, u32[]{:S(2)}) copy-start(bf16[384,384]{1,0:T(8,128)(2,1)S(1)} %get-tuple-element.1282) | copy-start | bytes 884740 | tf_op jit(solution)/shard_map/while
  434.0 31.4 %copy-start.64 = (f32[64]{0:T(128)}, f32[64]{0:T(128)S(1)}, u32[]{:S(2)}) copy-start(f32[64]{0:T(128)S(1)} %convert_element_type.425) | copy-start | bytes 772 | tf_op jit(solution)/shard_map/while
  435.7 9.6 copy-start.61
  436.3 9.0 copy-start.76
  444.0 52.3 %copy-start.2 = (bf16[1,1024,384]{1,2,0:T(8,128)(2,1)}, bf16[1,1024,384]{1,2,0:T(8,128)(2,1)S(1)}, u32[]{:S(2)}) copy-start(bf16[1,1024,384]{1,2,0:T(8,128)(2,1)S(1)} %copy.109) | copy-start | bytes 2359300 | tf_op jit(solution)/shard_map/while
  444.1 6.2 copy-start.50
  497.0 21.5 %copy-start.6 = (f32[1024,384]{0,1:T(8,128)}, f32[1024,384]{0,1:T(8,128)S(1)}, u32[]{:S(2)}) copy-start(f32[1024,384]{0,1:T(8,128)S(1)} %get-tuple-element.1077) | copy-start | bytes 4718596 | tf_op jit(solution)/shard_map/while
  497.9 15.3 %copy-start.22 = (bf16[1,1024,384]{2,1,0:T(8,128)(2,1)S(1)}, bf16[1,1024,384]{2,1,0:T(8,128)(2,1)}, u32[]{:S(2)}) copy-start(bf16[1,1024,384]{2,1,0:T(8,128)(2,1)} %copy-done.21) | copy-start | bytes 2359300 | tf_op jit(solution)/shard_map/while
  497.9 15.3 %copy-start.53 = (bf16[1536,384]{1,0:T(8,128)(2,1)S(1)}, bf16[1536,384]{1,0:T(8,128)(2,1)}, u32[]{:S(2)}) copy-start(bf16[1536,384]{1,0:T(8,128)(2,1)} %get-tuple-element.1288) | copy-start | bytes 3538948 | tf_op jit(solution)/shard_map/while
  556.4 51.3 %copy-start.32 = (f32[1024,6]{0,1:T(8,128)S(1)}, f32[1024,6]{0,1:T(8,128)}, u32[]{:S(2)}) copy-start(f32[1024,6]{0,1:T(8,128)} %copy-done.31) | copy-start | bytes 73732 | tf_op jit(solution)/shard_map/while
  556.4 51.4 %copy-start.65 = (f32[64]{0:T(128)S(1)}, f32[64]{0:T(128)}, u32[]{:S(2)}) copy-start(f32[64]{0:T(128)} %copy-done.64) | copy-start | bytes 772 | tf_op jit(solution)/shard_map/while
  562.6 7.2 copy-start.27
  587.1 7.2 copy-start.27
  723.2 174.7 %all-reduce.4.cloned.1.call-start = ((), (), s32[]{:S(2)}) async-start(), calls=%async_computation | async-start | bytes 3555328 | tf_op jit(solution)/shard_map/psum | solution.py:252
  725.0 172.9 %copy-start.41 = (f32[443776]{0:T(1024)S(1)}, f32[443776]{0:T(1024)}, u32[]{:S(2)}) copy-start(f32[443776]{0:T(1024)} %param.15) | copy-start | bytes 5325316
  725.0 172.8 %copy-start.52 = (f32[443776]{0:T(1024)S(1)}, f32[443776]{0:T(1024)}, u32[]{:S(2)}) copy-start(f32[443776]{0:T(1024)} %param.16) | copy-start | bytes 5325316
  801.5 165.1 %all-gather.7.cloned.1.call-start = ((), (), s32[]{:S(2)}) async-start(), calls=%async_computation.2 | async-start | bytes 8875520 | tf_op jit(solution)/shard_map/all_gather | solution.py:264
  (181 other events, 429.8 us)
Sparse Core Ops, SparseCore 0:
  19.8 53.6 all-gather.4
  723.3 75.2 all-reduce.5
  803.2 94.6 all-reduce.3
  915.1 51.4 all-gather.6
where the time goes:
time: 1050 us; the launch traced here: 1040 us
  local copies, waits for them, and re-layouts  283 us (27%)
  other arithmetic  272 us (26%)
  waiting for transfers between devices  233 us (22%)
  matrix products  187 us (18%)
  blocking collectives  40.9 us (4%)
  between operations  15 us (1%)
    concatenate x2, local copies, waits for them, and re-layouts, layer_pass(): return (output, input_grad, jnp.concatenate(pieces))  129 us
    psum x1, waiting for transfers between devices, shards(): owned_sum = lax.psum(owned_sum, 'dp')  96.4 us
    unnamed x5, waiting for transfers between devices  73.6 us
    all_gather x1, other arithmetic, shards(): lax.all_gather(master.astype(jnp.bfloat16), 'shard', axis=0, tiled=True)  64.1 us
    all_gather x1, other arithmetic, shards(): lax.all_gather(new_master.astype(jnp.bfloat16), 'shard', axis=0, tiled=True)  62.3 us
    all_gather x1, waiting for transfers between devices, shards(): lax.all_gather(master.astype(jnp.bfloat16), 'shard', axis=0, tiled=True)  53.6 us
    psum x1, blocking collectives, shards(): vector_sum = lax.psum(running[matrix_count:], ('dp', 'shard'))  40.9 us
    unnamed x39, local copies, waits for them, and re-layouts  31.7 us
  transfers between devices with their start and end apart: 4, of which 4 were waited for; matrix products, arithmetic and copies ran while one was open for 0% of the time, Pallas kernels for 0%

commit v1 on v0

v1 whole, which is shorter than its diff:
```python
import functools

import jax
import jax.numpy as jnp
from jax import lax
from jax.experimental import pallas as pl
from jax.experimental.pallas import tpu as pltpu
from jax.sharding import PartitionSpec as P

F32, BF16 = jnp.float32, jnp.bfloat16
MESH = pl.DeviceIdType.MESH
D, HEADS, HD, FF = 384, 6, 64, 1536
STEP = 3
PARAMS = 1775104
EPS = 1e-06
FAR = -1e30
BETA_ONE, BETA_TWO, RATE, DECAY, ADAM_EPS = 0.5, 0.5, 0.03, 0.1, 1e-08

LANES = 128
PAIRS = HEADS // 2
QKV_ROWS = 3 * D * D // LANES
OUT_ROWS = D * D // LANES
UP_ROWS = D * FF // LANES
MAT_ROWS = QKV_ROWS + OUT_ROWS + 2 * UP_ROWS
ALL_ROWS = PARAMS // LANES
QUARTER = ALL_ROWS // 4
KEPT = -(-QUARTER // 16) * 16
TAIL0 = QKV_ROWS
TAIL3 = 3408
VEC_AT = MAT_ROWS - 3 * QUARTER - TAIL3
NORM_GAIN, NORM_BIAS, QKV_BIAS, QUERY, KEY, OUT_BIAS, MLP_GAIN, MLP_BIAS, UP_BIAS, DOWN_BIAS = 0, 3, 6, 15, 16, 17, 20, 23, 26, 38
VMEM = 60 * 2**20


def dot(a, b):
    return jnp.dot(a, b, preferred_element_type=F32)


def dot_nt(a, b):
    return lax.dot_general(a, b, (((1,), (1,)), ((), ())), preferred_element_type=F32)


def dot_tn(a, b):
    return lax.dot_general(a, b, (((0,), (0,)), ((), ())), preferred_element_type=F32)


def row_of(vec, first, count):
    rows = [vec[VEC_AT + first + j : VEC_AT + first + j + 1, :] for j in range(count)]
    return jnp.concatenate(rows, axis=1) if count > 1 else rows[0]


def low_half(rows=1):
    return lax.broadcasted_iota(jnp.int32, (rows, LANES), 1) < HD


def both_halves(row, half):
    other = pltpu.roll(row, HD, 1)
    return jnp.where(low_half(), row, other) if half == 0 else jnp.where(low_half(), other, row)


def group_matrix(value, swapped=False):
    r = lax.rem(lax.broadcasted_iota(jnp.int32, (2 * LANES, LANES), 0), LANES) // HD
    c = lax.broadcasted_iota(jnp.int32, (2 * LANES, LANES), 1) // HD
    hit = (r != c) if swapped else (r == c)
    return jnp.where(hit, value, 0.0).astype(BF16)


def split(v):
    high = v.astype(BF16)
    return jnp.concatenate([high, (v - high.astype(F32)).astype(BF16)], axis=1)


def window(i, count):
    first, last = max(i - 1, 0), min(i + 2, count)
    return 256 * first, 256 * (last - first)


def columns(i, count):
    return sum(window(j, count)[1] for j in range(i))


def norm_stats(v):
    mean = jnp.mean(v, axis=1, keepdims=True)
    c = v - mean
    var = jnp.mean(c * c, axis=1, keepdims=True)
    r = lax.rsqrt(var + EPS)
    return c * r, r


def attn_forward_kernel(x_ref, qf_ref, kf_ref, w_ref, vec_ref, att_ref, e_ref, q_ref, k_ref, v_ref, xq_ref, xk_ref, rq_ref, rk_ref, it_ref, wp_ref, n_s, wf_s, ka_s, va_s):
    s, p = pl.program_id(0), pl.program_id(1)
    seq = x_ref.shape[1]
    blocks = seq // 256

    @pl.when((s == 0) & (p == 0))
    def _():
        wf_s[...] = w_ref[0, :QKV_ROWS].astype(F32)
        for j in range(PAIRS):
            for g in range(3):
                wp_ref[j, :, g * LANES : (g + 1) * LANES] = wf_s[pl.ds(3 * g + j, D, stride=9), :].astype(BF16)

    @pl.when(p == 0)
    def _():
        gain = row_of(vec_ref[...].astype(F32), NORM_GAIN, 3)
        bias = row_of(vec_ref[...].astype(F32), NORM_BIAS, 3)

        def body(i, carry):
            rows = pl.ds(pl.multiple_of(i * 256, 256), 256)
            xhat, _ = norm_stats(x_ref[0, rows, :].astype(F32))
            n_s[rows, :] = (xhat * gain + bias).astype(BF16)
            return carry

        lax.fori_loop(0, blocks, body, 0)

    vec = vec_ref[...].astype(F32)
    small = lax.broadcasted_iota(jnp.int32, (16, LANES), 0)
    qkv = vec[VEC_AT + QKV_BIAS : VEC_AT + QKV_BIAS + 9, :]
    which = lax.broadcasted_iota(jnp.int32, (9, LANES), 0)
    pick = lambda g: jnp.sum(jnp.where(which == 3 * g + p, qkv, 0.0), axis=0, keepdims=True)
    bias = jnp.concatenate([pick(0), pick(1), pick(2)], axis=1)
    qrow, krow = row_of(vec, QUERY, 1), row_of(vec, KEY, 1)
    qg, qb = both_halves(qrow, 0), both_halves(qrow, 1)
    kg, kb = both_halves(krow, 0), both_halves(krow, 1)
    means = group_matrix(1.0 / HD)
    w = wp_ref[p]

    def project(i, carry):
        rows = pl.ds(pl.multiple_of(i * 256, 256), 256)
        low = low_half(256)
        pr = dot(n_s[rows, :], w) + bias

        def head_norm(v):
            c = v - dot(split(v), means)
            r = lax.rsqrt(dot(split(c * c), means) + EPS)
            return c * r, r

        xq, rq = head_norm(pr[:, :LANES])
        xk, rk = head_norm(pr[:, LANES : 2 * LANES])
        q_ref[0, 0, rows, :] = ((xq * qg + qb) * HD**-0.5).astype(BF16)
        k = xk * kg + kb
        v = pr[:, 2 * LANES :]
        k_ref[0, 0, rows, :] = k.astype(BF16)
        v_ref[0, 0, rows, :] = v.astype(BF16)
        kf = kf_ref[0, rows, :].astype(F32)
        ka_s[0, rows, :] = jnp.where(low, k, kf).astype(BF16)
        ka_s[1, rows, :] = jnp.where(low, kf, k).astype(BF16)
        va_s[0, rows, :] = jnp.where(low, v, 1.0).astype(BF16)
        va_s[1, rows, :] = jnp.where(low, 1.0, v).astype(BF16)
        xq_ref[0, 0, rows, :] = xq.astype(BF16)
        xk_ref[0, 0, rows, :] = xk.astype(BF16)
        rq_ref[0, 0, rows, :] = rq
        rk_ref[0, 0, rows, :] = rk
        return carry

    lax.fori_loop(0, blocks, project, 0)

    low = low_half(256)
    for i in range(blocks):
        start, width = window(i, blocks)
        at = columns(i, blocks)
        rows = slice(256 * i, 256 * (i + 1))
        q = q_ref[0, 0, rows, :].astype(F32)
        qf = qf_ref[0, rows, :].astype(F32)
        sums = []
        for h in range(2):
            qa = (jnp.where(low, q, qf) if h == 0 else jnp.where(low, qf, q)).astype(BF16)
            scores = dot_nt(qa, ka_s[h, start : start + width, :])
            e = jnp.exp(scores - jnp.max(scores, axis=1, keepdims=True)).astype(BF16)
            e_ref[0, 0, 256 * h : 256 * (h + 1), at : at + width] = e
            sums.append(dot(e, va_s[h, start : start + width, :]))
        mixed = jnp.where(low, sums[0], sums[1])
        inverse = 1.0 / pltpu.roll(jnp.where(low, sums[1], sums[0]), HD, 1)
        att_ref[0, rows, :] = (mixed * inverse).astype(BF16)
        it_ref[0, 0, rows, :] = inverse


def attn_forward(x, qf, kf, weights, vec):
    seqs, seq, _ = x.shape
    total = columns(seq // 256, seq // 256)
    pair = lambda dtype: (jax.ShapeDtypeStruct((seqs, PAIRS, seq, LANES), dtype), pl.BlockSpec((1, 1, seq, LANES), lambda s, p: (s, p, 0, 0)))
    outs = [
        (jax.ShapeDtypeStruct((seqs, seq, D), BF16), pl.BlockSpec((1, seq, LANES), lambda s, p: (s, 0, p))),
        (jax.ShapeDtypeStruct((seqs, PAIRS, 512, total), BF16), pl.BlockSpec((1, 1, 512, total), lambda s, p: (s, p, 0, 0))),
        pair(BF16),
        pair(BF16),
        pair(BF16),
        pair(BF16),
        pair(BF16),
        pair(F32),
        pair(F32),
        pair(F32),
        (jax.ShapeDtypeStruct((PAIRS, D, D), BF16), pl.BlockSpec((PAIRS, D, D), lambda s, p: (0, 0, 0))),
    ]
    return pl.pallas_call(
        attn_forward_kernel,
        grid=(seqs, PAIRS),
        in_specs=[
            pl.BlockSpec((1, seq, D), lambda s, p: (s, 0, 0)),
            pl.BlockSpec((1, seq, LANES), lambda s, p: (s, 0, 0)),
            pl.BlockSpec((1, seq, LANES), lambda s, p: (s, 0, 0)),
            pl.BlockSpec((1, KEPT, LANES), lambda s, p: (0, 0, 0)),
            pl.BlockSpec(vec.shape, lambda s, p: (0, 0)),
        ],
        out_shape=[o[0] for o in outs],
        out_specs=[o[1] for o in outs],
        scratch_shapes=[
            pltpu.VMEM((seq, D), BF16),
            pltpu.VMEM((QKV_ROWS, LANES), F32),
            pltpu.VMEM((2, seq, LANES), BF16),
            pltpu.VMEM((2, seq, LANES), BF16),
        ],
        compiler_params=pltpu.CompilerParams(vmem_limit_bytes=VMEM),
        name="attn_forward",
    )(x, qf, kf, weights, vec)


def gelu_parts(x):
    bell = jnp.exp(x * x * -0.5)
    d = 1.0 + (0.3275911 * 0.5**0.5) * jnp.abs(x)
    t = pl.reciprocal(d, approx=True)
    t = t * (2.0 - d * t)
    poly = t * (0.127414796 + t * (-0.142248368 + t * (0.7107068705 + t * (-0.7265760135 + t * 0.5307027145))))
    tail = poly * bell
    share = jnp.where(x >= 0, 1.0 - tail, tail)
    return x * share, share + x * bell * 0.3989422804014327


def mlp_kernel(x_ref, att_ref, og_ref, w_ref, vec_ref, act_ref, mixed_ref, resid_ref, grads_ref, tail_ref, flat_s, wout_s, wup_s, wdown_s, mid_s, hid_s, pre_s, branch_s, colsum_s, upsum_s):
    t = pl.program_id(0)
    up_at, down_at = OUT_ROWS, OUT_ROWS + UP_ROWS
    step = KEPT // 7
    vec = vec_ref[...].astype(F32)
    tile = x_ref.shape[0]

    @pl.when(t == 0)
    def _():
        flat_s[0:16, :] = w_ref[0, TAIL0:KEPT].astype(F32)
        for k in range(1, 4):
            for c in range(7):
                at = k * QUARTER - QKV_ROWS + c * step
                count = min(step, flat_s.shape[0] - at)
                flat_s[at : at + count, :] = w_ref[k, c * step : (c + 1) * step].astype(F32)[:count]
        for j in range(3):
            wout_s[:, j * LANES : (j + 1) * LANES] = flat_s[pl.ds(j, D, stride=3), :].astype(BF16)
            wdown_s[:, j * LANES : (j + 1) * LANES] = flat_s[pl.ds(down_at + j, FF, stride=3), :].astype(BF16)
        for j in range(12):
            wup_s[:, j * LANES : (j + 1) * LANES] = flat_s[pl.ds(up_at + j, D, stride=12), :].astype(BF16)
        colsum_s[...] = jnp.zeros_like(colsum_s)
        upsum_s[...] = jnp.zeros_like(upsum_s)

    rows = pl.ds(pl.multiple_of(t * tile, tile), tile)
    fold = lambda v: jnp.sum(v.reshape(tile // 8, 8, v.shape[1]), axis=0)
    og = og_ref[rows, :]
    att = att_ref[rows, :]
    og_f = og.astype(F32)
    residual = x_ref[...].astype(F32) + dot(att, wout_s[...]) + row_of(vec, OUT_BIAS, 3)
    xhat, r = norm_stats(residual)
    gain = row_of(vec, MLP_GAIN, 3)
    mid = (xhat * gain + row_of(vec, MLP_BIAS, 3)).astype(BF16)
    mid_s[rows, :] = mid
    act = residual + row_of(vec, DOWN_BIAS, 3)
    mid_grad = jnp.zeros((tile, D), F32)
    wide = 512
    for c in range(FF // wide):
        cols = slice(c * wide, (c + 1) * wide)
        pre = dot(mid, wup_s[:, cols]) + row_of(vec, UP_BIAS + c * wide // LANES, wide // LANES)
        act_grad = dot_nt(og, wdown_s[cols, :])
        hidden, slope = gelu_parts(pre)
        hidden = hidden.astype(BF16)
        pre_grad = (act_grad * slope).astype(BF16)
        hid_s[rows, cols] = hidden
        pre_s[rows, cols] = pre_grad
        upsum_s[:, cols] += fold(pre_grad.astype(F32))
        act = act + dot(hidden, wdown_s[cols, :])
        mid_grad = mid_grad + dot_nt(pre_grad, wup_s[:, cols])
    act_ref[...] = act.astype(BF16)
    e_hat = mid_grad * gain
    resid = og_f + (e_hat - jnp.mean(e_hat, axis=1, keepdims=True) - xhat * jnp.mean(e_hat * xhat, axis=1, keepdims=True)) * r
    branch = resid.astype(BF16)
    resid_ref[...] = resid
    branch_s[rows, :] = branch
    mixed_ref[...] = dot_nt(branch, wout_s[...]).astype(BF16)
    colsum_s[0] += fold(og_f)
    colsum_s[1] += fold(mid_grad * xhat)
    colsum_s[2] += fold(mid_grad)
    colsum_s[3] += fold(branch.astype(F32))

    @pl.when(t == pl.num_programs(0) - 1)
    def _():
        for j in range(3):
            flat_s[pl.ds(j, D, stride=3), :] = dot_tn(att_ref[...], branch_s[:, j * LANES : (j + 1) * LANES])

        def ups(c, carry):
            g = dot_tn(mid_s[...], pre_s[:, pl.ds(pl.multiple_of(c * 256, 256), 256)])
            for j in range(2):
                flat_s[pl.ds(up_at + 2 * c + j, D, stride=12), :] = g[:, j * LANES : (j + 1) * LANES]
            return carry

        lax.fori_loop(0, FF // 256, ups, 0)

        def downs(c, carry):
            g = dot_tn(hid_s[:, pl.ds(pl.multiple_of(c * 256, 256), 256)], og_ref[...])
            for j in range(3):
                flat_s[pl.ds(down_at + 768 * c + j, 256, stride=3), :] = g[:, j * LANES : (j + 1) * LANES]
            return carry

        lax.fori_loop(0, FF // 256, downs, 0)
        sums = jnp.sum(colsum_s[...], axis=1)
        upsum = jnp.sum(upsum_s[...], axis=0, keepdims=True)
        vec_at = MAT_ROWS - QKV_ROWS
        flat_s[vec_at:, :] = jnp.zeros((flat_s.shape[0] - vec_at, LANES), F32)
        for j in range(3):
            part = slice(j * LANES, (j + 1) * LANES)
            flat_s[vec_at + DOWN_BIAS + j : vec_at + DOWN_BIAS + j + 1, :] = sums[0:1, part]
            flat_s[vec_at + MLP_GAIN + j : vec_at + MLP_GAIN + j + 1, :] = sums[1:2, part]
            flat_s[vec_at + MLP_BIAS + j : vec_at + MLP_BIAS + j + 1, :] = sums[2:3, part]
            flat_s[vec_at + OUT_BIAS + j : vec_at + OUT_BIAS + j + 1, :] = sums[3:4, part]
        for j in range(12):
            flat_s[vec_at + UP_BIAS + j : vec_at + UP_BIAS + j + 1, :] = upsum[:, j * LANES : (j + 1) * LANES]
        for k in range(1, 4):
            for c in range(7):
                at = k * QUARTER - QKV_ROWS + c * step
                grads_ref[k - 1, c * step : (c + 1) * step, :] = flat_s[at : at + step, :].astype(BF16)
        tail_ref[0:16, :] = flat_s[0:16, :]
        tail_ref[16:80, :] = flat_s[3 * QUARTER - QKV_ROWS + TAIL3 : 3 * QUARTER - QKV_ROWS + KEPT, :]


def mlp(x, att, og, weights, vec):
    tokens = x.shape[0]
    tile = 256
    padded = 3 * QUARTER + KEPT - QKV_ROWS
    tiled = pl.BlockSpec((tile, D), lambda t: (t, 0))
    whole = lambda *shape: pl.BlockSpec(shape, lambda t: (0,) * len(shape))
    return pl.pallas_call(
        mlp_kernel,
        grid=(tokens // tile,),
        in_specs=[tiled, whole(tokens, D), whole(tokens, D), whole(4, KEPT, LANES), whole(*vec.shape)],
        out_shape=[
            jax.ShapeDtypeStruct((tokens, D), BF16),
            jax.ShapeDtypeStruct((tokens, D), BF16),
            jax.ShapeDtypeStruct((tokens, D), F32),
            jax.ShapeDtypeStruct((3, KEPT, LANES), BF16),
            jax.ShapeDtypeStruct((80, LANES), F32),
        ],
        out_specs=[tiled, tiled, tiled, whole(3, KEPT, LANES), whole(80, LANES)],
        scratch_shapes=[
            pltpu.VMEM((padded, LANES), F32),
            pltpu.VMEM((D, D), BF16),
            pltpu.VMEM((D, FF), BF16),
            pltpu.VMEM((FF, D), BF16),
            pltpu.VMEM((tokens, D), BF16),
            pltpu.VMEM((tokens, FF), BF16),
            pltpu.VMEM((tokens, FF), BF16),
            pltpu.VMEM((tokens, D), BF16),
            pltpu.VMEM((4, 8, D), F32),
            pltpu.VMEM((8, FF), F32),
        ],
        compiler_params=pltpu.CompilerParams(vmem_limit_bytes=VMEM),
        name="mlp",
    )(x, att, og, weights, vec)


def attn_backward_kernel(x_ref, resid_ref, mixed_ref, att_ref, e_ref, q_ref, k_ref, v_ref, xq_ref, xk_ref, rq_ref, rk_ref, it_ref, wp_ref, vec_ref, tail_ref, gin_ref, grad_ref, tail_out_ref, n_s, in_s, dq_s, dk_s, dv_s, va_s, pg_s, acc_s, flat_s, sums_s, heads_s, bias_s):
    s, p = pl.program_id(0), pl.program_id(1)
    seq = x_ref.shape[1]
    blocks = seq // 256
    vec = vec_ref[...].astype(F32)
    fold = lambda v: jnp.sum(v.reshape(v.shape[0] // 8, 8, v.shape[1]), axis=0)
    low = low_half(256)

    @pl.when((s == 0) & (p == 0))
    def _():
        acc_s[...] = jnp.zeros_like(acc_s)
        sums_s[...] = jnp.zeros_like(sums_s)
        heads_s[...] = jnp.zeros_like(heads_s)
        bias_s[...] = jnp.zeros_like(bias_s)

    @pl.when(p == 0)
    def _():
        gain, bias = row_of(vec, NORM_GAIN, 3), row_of(vec, NORM_BIAS, 3)

        def body(i, carry):
            rows = pl.ds(pl.multiple_of(i * 256, 256), 256)
            xhat, _ = norm_stats(x_ref[0, rows, :].astype(F32))
            n_s[rows, :] = (xhat * gain + bias).astype(BF16)
            return carry

        lax.fori_loop(0, blocks, body, 0)

    dk_s[...] = jnp.zeros_like(dk_s)
    dv_s[...] = jnp.zeros_like(dv_s)
    ones = jnp.ones((256, LANES), F32)
    for i in range(blocks):
        rows = slice(256 * i, 256 * (i + 1))
        v = v_ref[0, 0, rows, :].astype(F32)
        va_s[0, rows, :] = jnp.where(low, v, ones).astype(BF16)
        va_s[1, rows, :] = jnp.where(low, ones, v).astype(BF16)
    swapped = group_matrix(1.0, swapped=True)
    lane = lax.rem(lax.broadcasted_iota(jnp.int32, (256, LANES), 1), HD)
    for i in range(blocks):
        start, width = window(i, blocks)
        at = columns(i, blocks)
        rows = slice(256 * i, 256 * (i + 1))
        keys = slice(start, start + width)
        do = (mixed_ref[0, rows, :].astype(F32) * it_ref[0, 0, rows, :]).astype(BF16).astype(F32)
        inner = dot(split(do * att_ref[0, rows, :].astype(F32)), swapped)
        high = inner.astype(BF16).astype(F32)
        extra = jnp.where(lane == 0, -high, jnp.where(lane == 1, high - inner, 0.0))
        q = q_ref[0, 0, rows, :].astype(F32)
        zero = jnp.zeros_like(q)
        dqs, dk, dv = [], None, None
        for h in range(2):
            mine = (lambda a, b: jnp.where(low, a, b).astype(BF16)) if h == 0 else (lambda a, b: jnp.where(low, b, a).astype(BF16))
            e = e_ref[0, 0, 256 * h : 256 * (h + 1), at : at + width]
            de = dot_nt(mine(do, extra), va_s[h, keys, :])
            ds = e * de.astype(BF16)
            dqs.append(dot(ds, k_ref[0, 0, keys, :]))
            dk_h = dot_tn(ds, mine(q, zero))
            dv_h = dot_tn(e, mine(do, zero))
            dk, dv = (dk_h, dv_h) if h == 0 else (dk + dk_h, dv + dv_h)
        dq_s[rows, :] = jnp.where(low, dqs[0], dqs[1]) * HD**-0.5
        dk_s[keys, :] += dk
        dv_s[keys, :] += dv

    qrow, krow = row_of(vec, QUERY, 1), row_of(vec, KEY, 1)
    qg, kg = both_halves(qrow, 0), both_halves(krow, 0)
    means = group_matrix(1.0 / HD)

    def pull(i, carry):
        rows = pl.ds(pl.multiple_of(i * 256, 256), 256)
        dq, dk, dv = dq_s[rows, :], dk_s[rows, :], dv_s[rows, :]

        def back(d, xhat, r, g):
            e_hat = d * g
            return (e_hat - dot(split(e_hat), means) - xhat * dot(split(e_hat * xhat), means)) * r

        xq, xk = xq_ref[0, 0, rows, :].astype(F32), xk_ref[0, 0, rows, :].astype(F32)
        heads_s[0] += fold(dq * xq)
        heads_s[1] += fold(dq)
        heads_s[2] += fold(dk * xk)
        heads_s[3] += fold(dk)
        pg = jnp.concatenate([back(dq, xq, rq_ref[0, 0, rows, :], qg), back(dk, xk, rk_ref[0, 0, rows, :], kg), dv], axis=1).astype(BF16)
        pg_s[rows, :] = pg
        bias_s[p] += fold(pg.astype(F32))
        share = dot_nt(pg, wp_ref[p])

        @pl.when(p == 0)
        def _():
            in_s[rows, :] = share

        @pl.when(p > 0)
        def _():
            in_s[rows, :] += share

        return carry

    lax.fori_loop(0, blocks, pull, 0)
    acc_s[p] += dot_tn(n_s[...], pg_s[...])

    @pl.when(p == PAIRS - 1)
    def _():
        gain = row_of(vec, NORM_GAIN, 3)

        def body(i, carry):
            rows = pl.ds(pl.multiple_of(i * 256, 256), 256)
            xhat, r = norm_stats(x_ref[0, rows, :].astype(F32))
            d = in_s[rows, :]
            e_hat = d * gain
            back = (e_hat - jnp.mean(e_hat, axis=1, keepdims=True) - xhat * jnp.mean(e_hat * xhat, axis=1, keepdims=True)) * r
            gin_ref[0, rows, :] = (resid_ref[0, rows, :] + back).astype(BF16)
            sums_s[0] += fold(d * xhat)
            sums_s[1] += fold(d)
            return carry

        lax.fori_loop(0, blocks, body, 0)

    @pl.when((s == pl.num_programs(0) - 1) & (p == PAIRS - 1))
    def _():
        for j in range(PAIRS):
            for g in range(3):
                flat_s[pl.ds(3 * g + j, D, stride=9), :] = acc_s[j, :, g * LANES : (g + 1) * LANES]
        grad_ref[0:TAIL0, :] = flat_s[...].astype(BF16)
        grad_ref[TAIL0:KEPT, :] = tail_ref[0:16, :].astype(BF16)
        tail_out_ref[...] = tail_ref[16:80, :]
        sums = jnp.sum(sums_s[...], axis=1)
        heads = jnp.sum(heads_s[...], axis=1)
        heads = heads + pltpu.roll(heads, HD, 1)
        biases = jnp.sum(bias_s[...], axis=1)

        def put(row, value):
            tail_out_ref[VEC_AT + row : VEC_AT + row + 1, :] = value

        for j in range(3):
            part = slice(j * LANES, (j + 1) * LANES)
            put(NORM_GAIN + j, sums[0:1, part])
            put(NORM_BIAS + j, sums[1:2, part])
            for g in range(3):
                put(QKV_BIAS + 3 * g + j, biases[j : j + 1, g * LANES : (g + 1) * LANES])
        put(QUERY, jnp.where(low_half(), heads[0:1], heads[1:2]))
        put(KEY, jnp.where(low_half(), heads[2:3], heads[3:4]))


def attn_backward(x, resid, mixed, att, e, q, k, v, xq, xk, rq, rk, it, wp, vec, tail):
    seqs, seq, _ = x.shape
    total = e.shape[-1]
    pair = pl.BlockSpec((1, 1, seq, LANES), lambda s, p: (s, p, 0, 0))
    whole = lambda *shape: pl.BlockSpec(shape, lambda s, p: (0,) * len(shape))
    full = pl.BlockSpec((1, seq, D), lambda s, p: (s, 0, 0))
    return pl.pallas_call(
        attn_backward_kernel,
        grid=(seqs, PAIRS),
        in_specs=[
            full,
            full,
            pl.BlockSpec((1, seq, LANES), lambda s, p: (s, 0, p)),
            pl.BlockSpec((1, seq, LANES), lambda s, p: (s, 0, p)),
            pl.BlockSpec((1, 1, 512, total), lambda s, p: (s, p, 0, 0)),
            pair,
            pair,
            pair,
            pair,
            pair,
            pair,
            pair,
            pair,
            whole(PAIRS, D, D),
            whole(*vec.shape),
            whole(80, LANES),
        ],
        out_shape=[
            jax.ShapeDtypeStruct((seqs, seq, D), BF16),
            jax.ShapeDtypeStruct((KEPT, LANES), BF16),
            jax.ShapeDtypeStruct((64, LANES), F32),
        ],
        out_specs=[full, whole(KEPT, LANES), whole(64, LANES)],
        scratch_shapes=[
            pltpu.VMEM((seq, D), BF16),
            pltpu.VMEM((seq, D), F32),
            pltpu.VMEM((seq, LANES), F32),
            pltpu.VMEM((seq, LANES), F32),
            pltpu.VMEM((seq, LANES), F32),
            pltpu.VMEM((2, seq, LANES), BF16),
            pltpu.VMEM((seq, D), BF16),
            pltpu.VMEM((PAIRS, D, D), F32),
            pltpu.VMEM((QKV_ROWS, LANES), F32),
            pltpu.VMEM((2, 8, D), F32),
            pltpu.VMEM((4, 8, LANES), F32),
            pltpu.VMEM((PAIRS, 8, D), F32),
        ],
        compiler_params=pltpu.CompilerParams(vmem_limit_bytes=VMEM),
        name="attn_backward",
    )(x, resid, mixed, att, e, q, k, v, xq, xk, rq, rk, it, wp, vec, tail)


def shards(patches, segments, out_grad, master, moment_one, moment_two):
    seqs, seq, _ = patches.shape
    rows = master.reshape(QUARTER, LANES).astype(BF16)
    rows = jnp.pad(rows, ((0, KEPT - QUARTER), (0, 0)))
    weights = lax.all_gather(rows, "shard", axis=0, tiled=False)
    vec = weights[3, TAIL3:KEPT]
    slot = jnp.arange(LANES, dtype=jnp.int32) % HD
    same = segments[:, :, None] == slot
    qf = jnp.where((slot < 8) & ~same, 1.0, 0.0).astype(BF16)
    kf = jnp.where((slot < 8) & same, FAR, 0.0).astype(BF16)
    att, e, q, k, v, xq, xk, rq, rk, it, wp = attn_forward(patches, qf, kf, weights, vec)
    flat = lambda a: a.reshape(seqs * seq, D)
    act, mixed, resid, grads, tail = mlp(flat(patches), flat(att), flat(out_grad), weights, vec)
    whole = lambda a: a.reshape(seqs, seq, D)
    input_grad, first, vec_tail = attn_backward(patches, whole(resid), whole(mixed), att, e, q, k, v, xq, xk, rq, rk, it, wp, vec, tail)
    sequences = seqs * lax.axis_size("dp") * lax.axis_size("shard")
    grads = grads.at[2, TAIL3:].set(vec_tail.astype(BF16))
    grads = jnp.concatenate([first[None], grads], axis=0)
    vector_grad = lax.psum(vec_tail, ("dp", "shard"))[VEC_AT : VEC_AT + ALL_ROWS - MAT_ROWS].reshape(-1) / sequences
    owned = lax.psum_scatter(grads, "shard", scatter_dimension=0, tiled=False).astype(F32)
    owned = lax.psum(owned, "dp")
    grad_sum = owned[:QUARTER].reshape(-1) / sequences
    first_moment = BETA_ONE * moment_one + (1.0 - BETA_ONE) * grad_sum
    second_moment = BETA_TWO * moment_two + (1.0 - BETA_TWO) * grad_sum * grad_sum
    first_hat = first_moment / (1.0 - BETA_ONE**STEP)
    second_hat = second_moment / (1.0 - BETA_TWO**STEP)
    positions = lax.axis_index("shard") * QUARTER * LANES + jnp.arange(QUARTER * LANES, dtype=jnp.int32)
    mask = (positions < MAT_ROWS * LANES).astype(F32)
    new_master = master - RATE * (first_hat / (jnp.sqrt(second_hat) + ADAM_EPS) + DECAY * mask * master)
    weights_copy = lax.all_gather(new_master.astype(BF16), "shard", axis=0, tiled=True)
    return whole(act), input_grad, grad_sum, vector_grad, new_master, first_moment, second_moment, weights_copy


def solution(mesh):
    split_rows = P(("dp", "shard"), None, None)
    return jax.shard_map(
        shards,
        mesh=mesh,
        in_specs=(split_rows, P(("dp", "shard"), None), split_rows, P("shard"), P("shard"), P("shard")),
        out_specs=(split_rows, split_rows, P("shard"), P(), P("shard"), P("shard"), P("shard"), P()),
        check_vma=False,
    )
```

time: 1050 us -> 470 us (0.45)
  local copies, waits for them, and re-layouts: 283 us -> 17.4 us
  other arithmetic: 272 us -> 78.6 us
  matrix products: 187 us -> 0 us
  Pallas kernels: 0 us -> 139 us
  waiting for transfers between devices: 233 us -> 180 us
    dot_general x52 -> x0, matrix products: 187 us -> none  [the longest x2 30.7 us: layer_pass(): jnp.dot(mid_low, params['up_weight'], preferred_element_type=jnp.float32)]
    pallas_call x0 -> x3, Pallas kernels: none -> 139 us  [the longest x1 52 us: attn_backward(): pl.pallas_call(attn_backward_kernel, grid=(seqs, PAIRS), in_specs=[full,...]
    concatenate x2 -> x0, local copies, waits for them, and re-layouts: 129 us -> none  [layer_pass(): return (output, input_grad, jnp.concatenate(pieces))]
    unnamed x5 -> x4, waiting for transfers between devices: 73.6 us -> 0.07 us
    all_gather x2 -> x1, other arithmetic: 126 us -> 62.3 us  [shards(): lax.all_gather(new_master.astype(BF16), 'shard', axis=0, tiled=True)]
    reduce_sum x34 -> x0, other arithmetic: 58.1 us -> none  [the longest x12 28.5 us: layer_norm(): return centered * lax.rsqrt(variance + NORM_EPS) * gain_vec + bias_vec]
    convert_element_type x36 -> x4, other arithmetic: 59.4 us -> 11.7 us  [the longest x1 6.23 us: shards(): new_master.astype(BF16)]
    reduce_scatter x0 -> x1, waiting for transfers between devices: none -> 40.6 us  [shards(): lax.psum_scatter(grads, 'shard', scatter_dimension=0, tiled=False)]
where the time goes in v1:
time: 470 us
  waiting for transfers between devices  180 us (38%)
  Pallas kernels  139 us (30%)
  other arithmetic  78.6 us (17%)
  blocking collectives  40.9 us (9%)
  local copies, waits for them, and re-layouts  17.4 us (4%)
  between operations  13.9 us (3%)
    psum x1, waiting for transfers between devices, shards(): owned = lax.psum(owned, 'dp')  96.7 us
    all_gather x1, other arithmetic, shards(): lax.all_gather(new_master.astype(BF16), 'shard', axis=0, tiled=True)  62.3 us
    pallas_call x1, Pallas kernels, attn_backward(): pl.pallas_call(attn_backward_kernel, grid=(seqs, PAIRS), in_specs=[full,...  52 us
    pallas_call x1, Pallas kernels, mlp(): pl.pallas_call(mlp_kernel, grid=(tokens // tile,), in_specs=[tiled, whole...  46.6 us
    psum x1, blocking collectives, shards(): lax.psum(vec_tail, ('dp', 'shard'))[VEC_AT:VEC_AT + ALL_ROWS - MAT_ROWS]  40.9 us
    reduce_scatter x1, waiting for transfers between devices, shards(): lax.psum_scatter(grads, 'shard', scatter_dimension=0, tiled=False)  40.6 us
    pallas_call x1, Pallas kernels, attn_forward(): pl.pallas_call(attn_forward_kernel, grid=(seqs, PAIRS), in_specs=[pl.Bloc...  40.4 us
    all_gather x1, waiting for transfers between devices, shards(): weights = lax.all_gather(rows, 'shard', axis=0, tiled=False)  32.5 us
  transfers between devices with their start and end apart: 4, of which 4 were waited for; matrix products, arithmetic and copies ran while one was open for 0% of the time, Pallas kernels for 0%

profile of v1, /device:TPU:0, one launch (start us, length us, event | category | flops | bytes accessed | tf_op | source)
XLA Modules:
  0.0 469.8 jit_solution(8164361100306153822)
XLA Ops:
  7.2 0.0 all-gather.5.cloned.1.call-start
  7.2 1.6 convert_bitcast_fusion
  8.8 0.0 copy-start.4
  8.8 1.0 pad.8
  9.8 0.0 all-gather.5.cloned.1.call-update
  9.8 0.0 reduce-scatter.2.cloned.1.call-start
  9.9 1.4 select_convert_fusion
  11.3 32.5 %all-gather.5.cloned.1.call-done = bf16[13888,128]{1,0:T(8,128)(2,1)} async-done(((bf16[3472,128]{1,0:T(8,128)(2,1)}), bf16[13888,128]{1,0:T(8,128)(2,1)}) %all-gather.5.cloned.1.call-update) | async-done | bytes 3555344 | tf_op jit(solution)/shard_map/all_gather | solution.py:559
  43.7 1.3 slice_bitcast_fusion.vec_ref
  45.1 40.4 %attn_forward.1 = (bf16[2,1024,384]{2,1,0:T(8,128)(2,1)}, bf16[2,3,512,2560]{3,2,1,0:T(8,128)(2,1)}, bf16[2,3,1024,128]{3,2,1,0:T(8,128)(2,1)}, bf16[2,3,1024,12...) custom-call(bf16[2,1024,384]{2,1,0:T(8,128)(2,1)} %x_ref.3, ...), custom_call_target="tpu_custom_call" | custom-call | tf_op jit(solution)/shard_map/attn_forward/pallas_call | solution.py:194
  85.4 46.6 %mlp.1 = (bf16[2048,384]{1,0:T(8,128)(2,1)}, bf16[2048,384]{1,0:T(8,128)(2,1)}, f32[2048,384]{1,0:T(8,128)}, bf16[3,3472,128]{2,1,0:T(8,128)(2,1)}, f32[80,128]{1,0:T(8,128)}) custom-call(bf16[2048,384]{1,0:T(8,128)(2,1)} %bitcast.32, bf16[2048,384]{1,0:T(8,128)(2,1)} %bitcast.33, bf16[2048,384]{1,0:T(8,128)(2,1)} %bitcast.35, ...), custom_call_target="tpu_custom_call" | custom-call | tf_op jit(solution)/shard_map/mlp/pallas_call | solution.py:334
  132.0 0.0 copy-start.1
  132.0 52.0 %attn_backward.1 = (bf16[2,1024,384]{2,1,0:T(8,128)(2,1)}, bf16[3472,128]{1,0:T(8,128)(2,1)}, f32[64,128]{1,0:T(8,128)}) custom-call(bf16[2,1024,384]{2,1,0:T(8,128)(2,1)} %x_ref.3, f32[2,1024,384]{2,1,0:T(8,128)} %bitcast.34, bf16[2,1024,384]{2,1,0:T(8,128)(2,1)} %bitcast.36, bf16[2,1024,384]{2,1,0:T(8,128)(2,1)} %get-tuple-element.39.att_ref, ...), custom_call_target="tpu_custom_call" | custom-call | tf_op jit(solution)/shard_map/attn_backward/pallas_call | solution.py:509
  184.1 0.8 bitcast_dynamic-update-slice_fusion
  184.8 3.2 pad_maximum_fusion
  188.1 0.0 reduce-scatter.2.cloned.1.call-update
  188.1 0.0 copy-start
  188.1 0.0 copy-start.2
  188.1 0.0 all-reduce.3.cloned.1.call-start
  188.2 40.6 %reduce-scatter.2.cloned.1.call-done = bf16[1,3472,128]{2,1,0:T(8,128)(2,1)} async-done(((bf16[4,3472,128]{2,1,0:T(8,128)(2,1)}), bf16[1,3472,128]{2,1,0:T(8,128)(2,1)}) %reduce-scatter.2.cloned.1.call-update) | async-done | bytes 888848 | tf_op jit(solution)/shard_map/reduce_scatter | solution.py:574
  228.7 2.5 bitcast_convert_fusion
  231.2 0.0 all-reduce.3.cloned.1.call-update
  231.3 0.0 all-gather.7.cloned.1.call-start
  231.3 96.7 %all-reduce.3.cloned.1.call-done = f32[3472,128]{1,0:T(8,128)} async-done(((f32[3472,128]{1,0:T(8,128)}), f32[3472,128]{1,0:T(8,128)}) %all-reduce.3.cloned.1.call-update) | async-done | bytes 1777680 | tf_op jit(solution)/shard_map/psum | solution.py:575
  328.0 6.2 %fusion.3 = (bf16[443776]{0:T(1024)(128)(2,1)S(1)}, f32[443776]{0:T(1024)}, f32[443776]{0:T(1024)}, f32[443776]{0:T(1024)}, f32[443776]{0:T(1024)}) fusion(f32[443776]{0:T(1024)S(1)} %copy-done, s32[]{:T(128)S(6)} %mul.43, f32[3472,128]{1,0:T(8,128)} %all-reduce.3.cloned.1.call-done, f32[443776]{0:T(1024)S(1)} %copy-done.2, f32[443776]{0:T(1024)} %param.13), kind=kLoop, calls=%fused_computation.21 | loop fusion | flops 8431744 | bytes 15088388 | tf_op jit(solution)/shard_map/convert_element_type | solution.py:584
  334.3 10.8 %reshape.107 = bf16[1,1,443776]{2,1,0:T(2,128)(2,1)} reshape(bf16[443776]{0:T(1024)(128)(2,1)S(1)} %get-tuple-element.58) | data formatting | bytes 1775104
  345.1 0.0 all-gather.7.cloned.1.call-update
  345.1 40.9 %psum.15 = f32[64,128]{1,0:T(8,128)S(1)} all-reduce(f32[64,128]{1,0:T(8,128)S(1)} %copy-done.3), channel_id=1, replica_groups=mesh['dp'=8,'shard'=4] {'dp','shard'}, use_global_device_ids=true, to_apply=%region_2.3 | all-reduce | flops 8192 | bytes 65536 | tf_op jit(solution)/shard_map/psum | solution.py:573
  386.0 0.6 fusion.2
  386.6 10.1 %all-gather.7.cloned.1.call-done = bf16[4,1,443776]{2,1,0:T(2,128)(2,1)} async-done(((bf16[1,1,443776]{2,1,0:T(2,128)(2,1)}), bf16[4,1,443776]{2,1,0:T(2,128)(2,1)}) %all-gather.7.cloned.1.call-update) | async-done | bytes 3550224 | tf_op jit(solution)/shard_map/all_gather | solution.py:584
  396.7 62.3 %reduce.2 = bf16[4,443776]{1,0:T(4,128)(2,1)S(1)} reduce(bf16[4,1,443776]{2,1,0:T(2,128)(2,1)} %all-gather.7.cloned.1.call-done, bf16[]{:T(256)} %constant.95), dimensions={1}, to_apply=%all-gather.1.reduce_sub_computation | reduce | bytes 7100418 | tf_op jit(solution)/shard_map/all_gather | solution.py:584
  459.0 4.3 reshape.108
  (8 shorter events, 0.0 us)
Async XLA Ops:
  7.2 36.6 %all-gather.5.cloned.1.call-start = ((), (), s32[]{:S(2)}) async-start(), calls=%async_computation.3 | async-start | bytes 4444160 | tf_op jit(solution)/shard_map/all_gather | solution.py:559
  8.8 1.1 copy-start.4
  9.8 218.9 %reduce-scatter.2.cloned.1.call-start = ((), (), s32[]{:S(2)}) async-start(), calls=%async_computation.1 | async-start | bytes 4444160 | tf_op jit(solution)/shard_map/reduce_scatter | solution.py:574
  132.0 52.1 %copy-start.1 = (bf16[3,3472,128]{2,1,0:T(8,128)(2,1)S(1)}, bf16[3,3472,128]{2,1,0:T(8,128)(2,1)}, u32[]{:S(2)}) copy-start(bf16[3,3472,128]{2,1,0:T(8,128)(2,1)} %get-tuple-element.56) | copy-start | bytes 7999492
  188.1 139.9 %copy-start = (f32[443776]{0:T(1024)S(1)}, f32[443776]{0:T(1024)}, u32[]{:S(2)}) copy-start(f32[443776]{0:T(1024)} %param.11) | copy-start | bytes 5325316
  188.1 139.9 %copy-start.2 = (f32[443776]{0:T(1024)S(1)}, f32[443776]{0:T(1024)}, u32[]{:S(2)}) copy-start(f32[443776]{0:T(1024)} %param.12) | copy-start | bytes 5325316
  188.1 139.9 %all-reduce.3.cloned.1.call-start = ((), (), s32[]{:S(2)}) async-start(), calls=%async_computation.2 | async-start | bytes 3555328 | tf_op jit(solution)/shard_map/psum | solution.py:575
  231.3 165.5 %all-gather.7.cloned.1.call-start = ((), (), s32[]{:S(2)}) async-start(), calls=%async_computation.4 | async-start | bytes 8875520 | tf_op jit(solution)/shard_map/all_gather | solution.py:584
  334.3 10.9 %copy-start.3 = (f32[64,128]{1,0:T(8,128)S(1)}, f32[64,128]{1,0:T(8,128)}, u32[]{:S(2)}) copy-start(f32[64,128]{1,0:T(8,128)} %get-tuple-element.57) | copy-start | bytes 98308
Sparse Core Ops, SparseCore 0:
  10.1 33.5 all-gather.4
  188.2 40.4 reduce-scatter.1
  233.4 94.5 all-reduce.2
  345.3 51.4 all-gather.6

commit v2 on v1

--- a/solution.py
+++ b/solution.py
@@ -198,7 +198,7 @@
             pl.BlockSpec((1, seq, D), lambda s, p: (s, 0, 0)),
             pl.BlockSpec((1, seq, LANES), lambda s, p: (s, 0, 0)),
             pl.BlockSpec((1, seq, LANES), lambda s, p: (s, 0, 0)),
-            pl.BlockSpec((1, KEPT, LANES), lambda s, p: (0, 0, 0)),
+            pl.BlockSpec((1, QKV_ROWS, LANES), lambda s, p: (0, 0, 0)),
             pl.BlockSpec(vec.shape, lambda s, p: (0, 0)),
         ],
         out_shape=[o[0] for o in outs],
@@ -320,7 +320,9 @@
         for k in range(1, 4):
             for c in range(7):
                 at = k * QUARTER - QKV_ROWS + c * step
-                grads_ref[k - 1, c * step : (c + 1) * step, :] = flat_s[at : at + step, :].astype(BF16)
+                grads_ref[k, c * step : (c + 1) * step, :] = flat_s[at : at + step, :].astype(BF16)
+            if grads_ref.shape[1] > KEPT:
+                grads_ref[k, KEPT:, :] = jnp.zeros((grads_ref.shape[1] - KEPT, LANES), BF16)
         tail_ref[0:16, :] = flat_s[0:16, :]
         tail_ref[16:80, :] = flat_s[3 * QUARTER - QKV_ROWS + TAIL3 : 3 * QUARTER - QKV_ROWS + KEPT, :]
 
@@ -334,15 +336,15 @@
     return pl.pallas_call(
         mlp_kernel,
         grid=(tokens // tile,),
-        in_specs=[tiled, whole(tokens, D), whole(tokens, D), whole(4, KEPT, LANES), whole(*vec.shape)],
+        in_specs=[tiled, whole(tokens, D), whole(tokens, D), whole(*weights.shape), whole(*vec.shape)],
         out_shape=[
             jax.ShapeDtypeStruct((tokens, D), BF16),
             jax.ShapeDtypeStruct((tokens, D), BF16),
             jax.ShapeDtypeStruct((tokens, D), F32),
-            jax.ShapeDtypeStruct((3, KEPT, LANES), BF16),
+            jax.ShapeDtypeStruct(weights.shape, BF16),
             jax.ShapeDtypeStruct((80, LANES), F32),
         ],
-        out_specs=[tiled, tiled, tiled, whole(3, KEPT, LANES), whole(80, LANES)],
+        out_specs=[tiled, tiled, tiled, whole(*weights.shape), whole(80, LANES)],
         scratch_shapes=[
             pltpu.VMEM((padded, LANES), F32),
             pltpu.VMEM((D, D), BF16),
@@ -360,7 +362,7 @@
     )(x, att, og, weights, vec)
 
 
-def attn_backward_kernel(x_ref, resid_ref, mixed_ref, att_ref, e_ref, q_ref, k_ref, v_ref, xq_ref, xk_ref, rq_ref, rk_ref, it_ref, wp_ref, vec_ref, tail_ref, gin_ref, grad_ref, tail_out_ref, n_s, in_s, dq_s, dk_s, dv_s, va_s, pg_s, acc_s, flat_s, sums_s, heads_s, bias_s):
+def attn_backward_kernel(x_ref, resid_ref, mixed_ref, att_ref, e_ref, q_ref, k_ref, v_ref, xq_ref, xk_ref, rq_ref, rk_ref, it_ref, wp_ref, vec_ref, tail_ref, old_ref, gin_ref, grads_ref, n_s, in_s, dq_s, dk_s, dv_s, va_s, pg_s, acc_s, flat_s, sums_s, heads_s, bias_s, first_s, tail_s, low_s, sems):
     s, p = pl.program_id(0), pl.program_id(1)
     seq = x_ref.shape[1]
     blocks = seq // 256
@@ -479,16 +481,20 @@
         for j in range(PAIRS):
             for g in range(3):
                 flat_s[pl.ds(3 * g + j, D, stride=9), :] = acc_s[j, :, g * LANES : (g + 1) * LANES]
-        grad_ref[0:TAIL0, :] = flat_s[...].astype(BF16)
-        grad_ref[TAIL0:KEPT, :] = tail_ref[0:16, :].astype(BF16)
-        tail_out_ref[...] = tail_ref[16:80, :]
+        first_s[0:TAIL0, :] = flat_s[...].astype(BF16)
+        first_s[TAIL0:KEPT, :] = tail_ref[0:16, :].astype(BF16)
+        if first_s.shape[0] > KEPT:
+            first_s[KEPT:, :] = jnp.zeros((first_s.shape[0] - KEPT, LANES), BF16)
+        first = pltpu.make_async_copy(first_s, grads_ref.at[0], sems.at[0])
+        first.start()
+        tail_s[...] = tail_ref[16:80, :]
         sums = jnp.sum(sums_s[...], axis=1)
         heads = jnp.sum(heads_s[...], axis=1)
         heads = heads + pltpu.roll(heads, HD, 1)
         biases = jnp.sum(bias_s[...], axis=1)
 
         def put(row, value):
-            tail_out_ref[VEC_AT + row : VEC_AT + row + 1, :] = value
+            tail_s[VEC_AT + row : VEC_AT + row + 1, :] = value
 
         for j in range(3):
             part = slice(j * LANES, (j + 1) * LANES)
@@ -498,9 +504,14 @@
                 put(QKV_BIAS + 3 * g + j, biases[j : j + 1, g * LANES : (g + 1) * LANES])
         put(QUERY, jnp.where(low_half(), heads[0:1], heads[1:2]))
         put(KEY, jnp.where(low_half(), heads[2:3], heads[3:4]))
-
-
-def attn_backward(x, resid, mixed, att, e, q, k, v, xq, xk, rq, rk, it, wp, vec, tail):
+        low_s[...] = tail_s[...].astype(BF16)
+        last = pltpu.make_async_copy(low_s, grads_ref.at[3, TAIL3:KEPT], sems.at[1])
+        last.start()
+        first.wait()
+        last.wait()
+
+
+def attn_backward(x, resid, mixed, att, e, q, k, v, xq, xk, rq, rk, it, wp, vec, tail, grads):
     seqs, seq, _ = x.shape
     total = e.shape[-1]
     pair = pl.BlockSpec((1, 1, seq, LANES), lambda s, p: (s, p, 0, 0))
@@ -526,13 +537,14 @@
             whole(PAIRS, D, D),
             whole(*vec.shape),
             whole(80, LANES),
+            pl.BlockSpec(memory_space=pl.ANY),
         ],
         out_shape=[
             jax.ShapeDtypeStruct((seqs, seq, D), BF16),
-            jax.ShapeDtypeStruct((KEPT, LANES), BF16),
-            jax.ShapeDtypeStruct((64, LANES), F32),
+            jax.ShapeDtypeStruct(grads.shape, BF16),
         ],
-        out_specs=[full, whole(KEPT, LANES), whole(64, LANES)],
+        out_specs=[full, pl.BlockSpec(memory_space=pl.ANY)],
+        input_output_aliases={16: 1},
         scratch_shapes=[
             pltpu.VMEM((seq, D), BF16),
             pltpu.VMEM((seq, D), F32),
@@ -546,17 +558,346 @@
             pltpu.VMEM((2, 8, D), F32),
             pltpu.VMEM((4, 8, LANES), F32),
             pltpu.VMEM((PAIRS, 8, D), F32),
+            pltpu.VMEM(grads.shape[1:], BF16),
+            pltpu.VMEM((64, LANES), F32),
+            pltpu.VMEM((64, LANES), BF16),
+            pltpu.SemaphoreType.DMA((2,)),
         ],
         compiler_params=pltpu.CompilerParams(vmem_limit_bytes=VMEM),
         name="attn_backward",
-    )(x, resid, mixed, att, e, q, k, v, xq, xk, rq, rk, it, wp, vec, tail)
+    )(x, resid, mixed, att, e, q, k, v, xq, xk, rq, rk, it, wp, vec, tail, grads)
+
+
+CHUNKS = 4
+
+
+def padded_rows(n):
+    unit = 16 * n * CHUNKS
+    return -(-QUARTER // unit) * unit
+
+
+def position():
+    dp, shard = lax.axis_index("dp"), lax.axis_index("shard")
+    return dp, shard, shard // 2, lax.rem(shard, 2), lax.rem(dp, 2)
+
+
+def flip(dp, bit):
+    return dp + (1 - 2 * lax.rem(dp // bit, 2)) * bit
+
+
+def greet(peers):
+    barrier = pltpu.get_barrier_semaphore()
+    for peer in peers:
+        pl.semaphore_signal(barrier, inc=1, device_id=peer, device_id_type=MESH)
+    pl.semaphore_wait(barrier, len(peers))
+
+
+class Spread:
+    def __init__(self, own, out, sends, recvs, own_sem):
+        dp, shard, y, core, x = position()
+        self.own, self.out, self.sends, self.recvs, self.own_sem = own, out, sends, recvs, own_sem
+        self.mine, self.across = shard, 2 * (1 - y) + core
+        self.beside, self.diagonal = 2 * y + 1 - core, 2 * (1 - y) + 1 - core
+        self.x = x
+        self.core_peer, self.y_peer, self.x_peer = (dp, self.beside), (dp, self.across), (flip(dp, 1), shard)
+        self.chunk = own.shape[0] // CHUNKS
+        self.half = self.chunk // 2
+
+    def rows(self, c, half=None):
+        if half is None:
+            return pl.ds(c * self.chunk, self.chunk)
+        return pl.ds(pl.multiple_of(c * self.chunk + half * self.half, 16), self.half)
+
+    def copy(self, c, kind, src, quarter, rows, peer):
+        return pltpu.make_async_remote_copy(src_ref=src, dst_ref=self.out.at[quarter, rows], send_sem=self.sends.at[c, kind], recv_sem=self.recvs.at[c, kind], device_id=peer, device_id_type=MESH)
+
+    def to_core(self, c):
+        return self.copy(c, 0, self.own.at[self.rows(c)], self.mine, self.rows(c), self.core_peer)
+
+    def to_y(self, c):
+        rows = self.rows(c, self.x)
+        return self.copy(c, 1, self.own.at[rows], self.mine, rows, self.y_peer)
+
+    def onward(self, c, kind):
+        rows = self.rows(c, 1 - self.x if kind == 4 else self.x)
+        return self.copy(c, kind, self.out.at[self.across, rows], self.across, rows, self.x_peer if kind == 2 else self.core_peer)
+
+    def start(self, c):
+        self.to_y(c).start()
+        self.to_core(c).start()
+        rows = self.rows(c)
+        pltpu.make_async_copy(self.own.at[rows], self.out.at[self.mine, rows], self.own_sem.at[c]).start()
+
+    def middle(self, c):
+        self.to_y(c).wait_recv()
+        self.onward(c, 2).start()
+        self.onward(c, 3).start()
+
+    def end(self, c):
+        self.onward(c, 2).wait_recv()
+        self.onward(c, 4).start()
+
+    def finish(self, c):
+        rows = self.rows(c)
+        pltpu.make_async_copy(self.own.at[rows], self.out.at[self.mine, rows], self.own_sem.at[c]).wait()
+        self.to_y(c).wait_send()
+        self.to_core(c).wait()
+        self.onward(c, 2).wait_send()
+        self.onward(c, 3).wait()
+        self.onward(c, 4).wait()
+
+
+def gather_kernel(master_ref, out_ref, own_s, sends, recvs, own_sem):
+    dp, shard, y, core, x = position()
+    spread = Spread(own_s, out_ref, sends, recvs, own_sem)
+    greet([spread.core_peer, spread.y_peer, spread.x_peer])
+    for c in range(CHUNKS):
+        first, last = c * spread.chunk, (c + 1) * spread.chunk
+        inside = max(min(last, QUARTER) - first, 0)
+        if inside:
+            own_s[first : first + inside, :] = master_ref[first : first + inside, :].astype(BF16)
+        if first + inside < last:
+            own_s[first + inside : last, :] = jnp.zeros((last - first - inside, LANES), BF16)
+        spread.start(c)
+    for c in range(CHUNKS + 1):
+        if c < CHUNKS:
+            spread.middle(c)
+        if c > 0:
+            spread.end(c - 1)
+    for c in range(CHUNKS):
+        spread.finish(c)
+
+
+def gather_weights(master, padded):
+    return pl.pallas_call(
+        gather_kernel,
+        in_specs=[pl.BlockSpec(memory_space=pltpu.VMEM)],
+        out_shape=jax.ShapeDtypeStruct((4, padded, LANES), BF16),
+        out_specs=pl.BlockSpec(memory_space=pl.ANY),
+        scratch_shapes=[
+            pltpu.VMEM((padded, LANES), BF16),
+            pltpu.SemaphoreType.DMA((CHUNKS, 5)),
+            pltpu.SemaphoreType.DMA((CHUNKS, 5)),
+            pltpu.SemaphoreType.DMA((CHUNKS,)),
+        ],
+        compiler_params=pltpu.CompilerParams(collective_id=0, has_side_effects=True, vmem_limit_bytes=VMEM),
+        name="gather_weights",
+    )(master)
+
+
+def adam(grad_sum, master, moment_one, moment_two, first_row):
+    first = BETA_ONE * moment_one + (1.0 - BETA_ONE) * grad_sum
+    second = BETA_TWO * moment_two + (1.0 - BETA_TWO) * grad_sum * grad_sum
+    first_hat = first * (1.0 / (1.0 - BETA_ONE**STEP))
+    second_hat = second * (1.0 / (1.0 - BETA_TWO**STEP))
+    row = first_row + lax.broadcasted_iota(jnp.int32, grad_sum.shape, 0)
+    decay = jnp.where(row < MAT_ROWS, DECAY, 0.0)
+    return first, second, master - RATE * (first_hat / (jnp.sqrt(second_hat) + ADAM_EPS) + decay * master)
+
+
+def reduce_kernel(n, scale, g_ref, master_ref, m1_ref, m2_ref, sum_ref, out_ref, vec_ref, pair_s, core_s, y_s, part_s, dp_s, all_s, new_s, vec_s, sends, recvs, loads, w_sends, w_recvs, own_sem, v_sends, v_recvs):
+    dp, shard, y, core, x = position()
+    bits = n.bit_length() - 1
+    spread = Spread(new_s, out_ref, w_sends, w_recvs, own_sem)
+    peers = [spread.core_peer, spread.y_peer] + [(flip(dp, 1 << b), shard) for b in range(bits)]
+    chunk = part_s.shape[1]
+    greet(peers)
+
+    def remote(c, kind, src, dst, peer):
+        return pltpu.make_async_remote_copy(src_ref=src, dst_ref=dst, send_sem=sends.at[c, kind], recv_sem=recvs.at[c, kind], device_id=peer, device_id_type=MESH)
+
+    def load(c, j):
+        return pltpu.make_async_copy(g_ref.at[2 * j + core, pl.ds(c * chunk, chunk)], pair_s.at[c, j], loads.at[c, j])
+
+    def to_core(c, j):
+        return remote(c, j, g_ref.at[2 * j + 1 - core, pl.ds(c * chunk, chunk)], core_s.at[c, j], peers[0])
+
+    def to_y(c):
+        return remote(c, 2, pair_s.at[c, 1 - y], y_s.at[c], peers[1])
+
+    def mine(b):
+        return lax.rem(dp // (1 << b), 2)
+
+    def offset(b):
+        return sum((mine(i) * (chunk >> (i + 1)) for i in range(b)), 0)
+
+    def piece(b, half):
+        size = chunk >> (b + 1)
+        return pl.ds(pl.multiple_of(offset(b) + half * size, 16), size)
+
+    def landing(b):
+        return pl.ds(chunk - (chunk >> b), chunk >> (b + 1))
+
+    def halve(c, b):
+        return remote(c, 3 + b, part_s.at[c, piece(b, 1 - mine(b))], dp_s.at[c, landing(b)], peers[2 + b])
+
+    def double(c, b):
+        at = piece(b, mine(b))
+        rows = pl.ds(pl.multiple_of(c * chunk + offset(b) + mine(b) * (chunk >> (b + 1)), 16), chunk >> (b + 1))
+        return remote(c, 3 + bits + b, all_s.at[rows], all_s.at[rows], peers[2 + b])
+
+    def add(a, b):
+        return (a.astype(F32) + b.astype(F32)).astype(BF16)
+
+    def stage(c, t):
+        if t == 0:
+            for j in range(2):
+                load(c, j).wait()
+                to_core(c, j).wait_recv()
+                pair_s[c, j] = add(pair_s[c, j], core_s[c, j])
+            to_y(c).start()
+        elif t == 1:
+            to_y(c).wait_recv()
+            part_s[c] = add(pair_s[c, y], y_s[c])
+            halve(c, 0).start()
+        elif t < 2 + bits:
+            b = t - 2
+            halve(c, b).wait_recv()
+            total = add(part_s[c, piece(b, mine(b)), :], dp_s[c, landing(b), :])
+            if b + 1 < bits:
+                part_s[c, piece(b, mine(b)), :] = total
+                halve(c, b + 1).start()
+            else:
+                rows = pl.ds(pl.multiple_of(c * chunk + offset(bits), 16), chunk >> bits)
+                all_s[rows, :] = total
+                double(c, bits - 1).start()
+        elif t < 2 + 2 * bits:
+            b = bits - 1 - (t - 2 - bits)
+            double(c, b).wait_recv()
+            if b > 0:
+                double(c, b - 1).start()
+            else:
+                update(c)
+                spread.start(c)
+        elif t == 2 + 2 * bits:
+            spread.middle(c)
+        elif t == 3 + 2 * bits:
+            spread.end(c)
+
+    def update(c):
+        first, last = c * chunk, (c + 1) * chunk
+        inside = max(min(last, QUARTER) - first, 0)
+        if inside:
+            rows = slice(first, first + inside)
+            grad = all_s[rows, :].astype(F32) * scale
+            new_s[rows, :] = adam(grad, master_ref[rows, :], m1_ref[rows, :], m2_ref[rows, :], shard * QUARTER + first)[2].astype(BF16)
+        if first + inside < last:
+            new_s[first + inside : last, :] = jnp.zeros((last - first - inside, LANES), BF16)
+
+    for c in range(CHUNKS):
+        for j in range(2):
+            to_core(c, j).start()
+            load(c, j).start()
+    stages = 4 + 2 * bits
+    for t in range(CHUNKS + stages - 1):
+        for c in range(CHUNKS):
+            if 0 <= t - c < stages:
+                stage(c, t - c)
+
+    def vectors(kind, quarter, peer):
+        return pltpu.make_async_remote_copy(src_ref=vec_s.at[quarter], dst_ref=vec_s.at[quarter], send_sem=v_sends.at[kind], recv_sem=v_recvs.at[kind], device_id=peer, device_id_type=MESH)
+
+    vec_s[spread.mine] = all_s[TAIL3:KEPT, :]
+    vectors(0, spread.mine, spread.core_peer).start()
+    vectors(1, spread.mine, spread.y_peer).start()
+    vectors(1, spread.mine, spread.y_peer).wait_recv()
+    vectors(2, spread.across, spread.core_peer).start()
+    sum_ref[...] = all_s[...]
+    for c in range(CHUNKS):
+        for j in range(2):
+            to_core(c, j).wait_send()
+        to_y(c).wait_send()
+        for b in range(bits):
+            halve(c, b).wait_send()
+            double(c, b).wait_send()
+        spread.finish(c)
+    vectors(0, spread.mine, spread.core_peer).wait()
+    vectors(1, spread.mine, spread.y_peer).wait_send()
+    vectors(2, spread.across, spread.core_peer).wait()
+    vec_ref[...] = vec_s[3].astype(F32) * scale
+
+
+def reduce_gradients(grads, master, moment_one, moment_two, n, sequences):
+    padded = grads.shape[1]
+    chunk = padded // CHUNKS
+    bits = n.bit_length() - 1
+    kinds = 3 + 2 * bits
+    anywhere, vmem = pl.BlockSpec(memory_space=pl.ANY), pl.BlockSpec(memory_space=pltpu.VMEM)
+    return pl.pallas_call(
+        functools.partial(reduce_kernel, n, 1.0 / sequences),
+        in_specs=[anywhere, vmem, vmem, vmem],
+        out_shape=[
+            jax.ShapeDtypeStruct((padded, LANES), BF16),
+            jax.ShapeDtypeStruct((4, padded, LANES), BF16),
+            jax.ShapeDtypeStruct((64, LANES), F32),
+        ],
+        out_specs=[vmem, anywhere, vmem],
+        scratch_shapes=[
+            pltpu.VMEM((CHUNKS, 2, chunk, LANES), BF16),
+            pltpu.VMEM((CHUNKS, 2, chunk, LANES), BF16),
+            pltpu.VMEM((CHUNKS, chunk, LANES), BF16),
+            pltpu.VMEM((CHUNKS, chunk, LANES), BF16),
+            pltpu.VMEM((CHUNKS, chunk, LANES), BF16),
+            pltpu.VMEM((padded, LANES), BF16),
+            pltpu.VMEM((padded, LANES), BF16),
+            pltpu.VMEM((4, 64, LANES), BF16),
+            pltpu.SemaphoreType.DMA((CHUNKS, kinds)),
+            pltpu.SemaphoreType.DMA((CHUNKS, kinds)),
+            pltpu.SemaphoreType.DMA((CHUNKS, 2)),
+            pltpu.SemaphoreType.DMA((CHUNKS, 5)),
+            pltpu.SemaphoreType.DMA((CHUNKS, 5)),
+            pltpu.SemaphoreType.DMA((CHUNKS,)),
+            pltpu.SemaphoreType.DMA((3,)),
+            pltpu.SemaphoreType.DMA((3,)),
+        ],
+        compiler_params=pltpu.CompilerParams(collective_id=1, has_side_effects=True, vmem_limit_bytes=VMEM),
+        name="reduce_gradients",
+    )(grads, master, moment_one, moment_two)
+
+
+UPDATE = 880
+
+
+def finish_kernel(scale, sum_ref, master_ref, m1_ref, m2_ref, w_ref, next_ref, grad_ref, new_ref, first_ref, second_ref, copy_ref):
+    b = pl.program_id(0)
+    grad = sum_ref[...].astype(F32) * scale
+    first, second, new = adam(grad, master_ref[...], m1_ref[...], m2_ref[...], lax.axis_index("shard") * QUARTER + b * UPDATE)
+    grad_ref[...], first_ref[...], second_ref[...], new_ref[...] = grad, first, second, new
+    for k in range(4):
+        skip = k * (KEPT - QUARTER)
+
+        @pl.when(b == k)
+        def _():
+            own = w_ref[0, :KEPT, :].astype(F32)
+            if k == 3:
+                copy_ref[...] = jnp.concatenate([own[skip:], own[:skip]], axis=0).astype(BF16)
+            else:
+                after = next_ref[0].astype(F32)
+                copy_ref[...] = jnp.concatenate([own[skip:QUARTER], after[: skip + KEPT - QUARTER]], axis=0).astype(BF16)
+
+
+def finish(sums, master, moment_one, moment_two, weights, sequences):
+    rows = lambda dtype: pl.BlockSpec((UPDATE, LANES), lambda b: (b, 0))
+    f32 = jax.ShapeDtypeStruct((QUARTER, LANES), F32)
+    padded = weights.shape[1]
+    return pl.pallas_call(
+        functools.partial(finish_kernel, 1.0 / sequences),
+        grid=(4,),
+        in_specs=[rows(BF16), rows(F32), rows(F32), rows(F32), pl.BlockSpec((1, padded, LANES), lambda b: (b, 0, 0)), pl.BlockSpec((1, 32, LANES), lambda b: (jnp.minimum(b + 1, 3), 0, 0))],
+        out_shape=[f32, f32, f32, f32, jax.ShapeDtypeStruct((ALL_ROWS, LANES), BF16)],
+        out_specs=[rows(F32), rows(F32), rows(F32), rows(F32), pl.BlockSpec((KEPT, LANES), lambda b: (b, 0))],
+        compiler_params=pltpu.CompilerParams(vmem_limit_bytes=VMEM),
+        name="finish",
+    )(sums, master, moment_one, moment_two, weights, weights)
 
 
 def shards(patches, segments, out_grad, master, moment_one, moment_two):
     seqs, seq, _ = patches.shape
-    rows = master.reshape(QUARTER, LANES).astype(BF16)
-    rows = jnp.pad(rows, ((0, KEPT - QUARTER), (0, 0)))
-    weights = lax.all_gather(rows, "shard", axis=0, tiled=False)
+    n = lax.axis_size("dp")
+    sequences = seqs * n * lax.axis_size("shard")
+    rows = lambda a: a.reshape(QUARTER, LANES)
+    master, moment_one, moment_two = rows(master), rows(moment_one), rows(moment_two)
+    weights = gather_weights(master, padded_rows(n))
     vec = weights[3, TAIL3:KEPT]
     slot = jnp.arange(LANES, dtype=jnp.int32) % HD
     same = segments[:, :, None] == slot
@@ -566,22 +907,11 @@
     flat = lambda a: a.reshape(seqs * seq, D)
     act, mixed, resid, grads, tail = mlp(flat(patches), flat(att), flat(out_grad), weights, vec)
     whole = lambda a: a.reshape(seqs, seq, D)
-    input_grad, first, vec_tail = attn_backward(patches, whole(resid), whole(mixed), att, e, q, k, v, xq, xk, rq, rk, it, wp, vec, tail)
-    sequences = seqs * lax.axis_size("dp") * lax.axis_size("shard")
-    grads = grads.at[2, TAIL3:].set(vec_tail.astype(BF16))
-    grads = jnp.concatenate([first[None], grads], axis=0)
-    vector_grad = lax.psum(vec_tail, ("dp", "shard"))[VEC_AT : VEC_AT + ALL_ROWS - MAT_ROWS].reshape(-1) / sequences
-    owned = lax.psum_scatter(grads, "shard", scatter_dimension=0, tiled=False).astype(F32)
-    owned = lax.psum(owned, "dp")
-    grad_sum = owned[:QUARTER].reshape(-1) / sequences
-    first_moment = BETA_ONE * moment_one + (1.0 - BETA_ONE) * grad_sum
-    second_moment = BETA_TWO * moment_two + (1.0 - BETA_TWO) * grad_sum * grad_sum
-    first_hat = first_moment / (1.0 - BETA_ONE**STEP)
-    second_hat = second_moment / (1.0 - BETA_TWO**STEP)
-    positions = lax.axis_index("shard") * QUARTER * LANES + jnp.arange(QUARTER * LANES, dtype=jnp.int32)
-    mask = (positions < MAT_ROWS * LANES).astype(F32)
-    new_master = master - RATE * (first_hat / (jnp.sqrt(second_hat) + ADAM_EPS) + DECAY * mask * master)
-    weights_copy = lax.all_gather(new_master.astype(BF16), "shard", axis=0, tiled=True)
+    input_grad, grads = attn_backward(patches, whole(resid), whole(mixed), att, e, q, k, v, xq, xk, rq, rk, it, wp, vec, tail, grads)
+    sums, weights, vectors = reduce_gradients(grads, master, moment_one, moment_two, n, sequences)
+    vector_grad = vectors[VEC_AT : VEC_AT + ALL_ROWS - MAT_ROWS].reshape(-1)
+    updated = finish(sums, master, moment_one, moment_two, weights, sequences)
+    grad_sum, new_master, first_moment, second_moment, weights_copy = [a.reshape(-1) for a in updated]
     return whole(act), input_grad, grad_sum, vector_grad, new_master, first_moment, second_moment, weights_copy
 
 

time: 470 us -> 250 us (0.53)
  waiting for transfers between devices: 180 us -> 0 us
  Pallas kernels: 139 us -> 245 us
  other arithmetic: 78.6 us -> 2.04 us
  blocking collectives: 40.9 us -> 0 us
  local copies, waits for them, and re-layouts: 17.4 us -> 2.69 us
  between operations: 13.9 us -> 0.68 us
    pallas_call x0 -> x3, Pallas kernels: none -> 105 us  [the longest x1 72.7 us: reduce_gradients(): pl.pallas_call(functools.partial(reduce_kernel, n, 1.0 / sequences), in_s...]
    psum x1 -> x0, waiting for transfers between devices: 96.7 us -> none  [shards(): owned = lax.psum(owned, 'dp')]
    all_gather x1 -> x0, other arithmetic: 62.3 us -> none  [shards(): lax.all_gather(new_master.astype(BF16), 'shard', axis=0, tiled=True)]
    all_gather x2 -> x0, waiting for transfers between devices: 42.6 us -> none  [the longest x1 32.5 us: shards(): weights = lax.all_gather(rows, 'shard', axis=0, tiled=False)]
    psum x1 -> x0, blocking collectives: 40.9 us -> none  [shards(): lax.psum(vec_tail, ('dp', 'shard'))[VEC_AT:VEC_AT + ALL_ROWS - MAT_ROWS]]
    reduce_scatter x1 -> x0, waiting for transfers between devices: 40.6 us -> none  [shards(): lax.psum_scatter(grads, 'shard', scatter_dimension=0, tiled=False)]
    unnamed x12 -> x0, local copies, waits for them, and re-layouts: 15.1 us -> none
    convert_element_type x3 -> x0, other arithmetic: 10.3 us -> none  [the longest x1 6.23 us: shards(): new_master.astype(BF16)]
  transfers between devices with their start and end apart: 4 -> 0, of which waited for: 4 -> 0; matrix products, arithmetic and copies ran while one was open for 0% -> 0% of each run, Pallas kernels for 0% -> 0%
where the time goes in v2:
time: 250 us
  Pallas kernels  245 us (98%)
  local copies, waits for them, and re-layouts  2.69 us (1%)
    pallas_call x1, Pallas kernels, reduce_gradients(): pl.pallas_call(functools.partial(reduce_kernel, n, 1.0 / sequences), in_s...  72.7 us
    pallas_call x1, Pallas kernels, attn_backward(): pl.pallas_call(attn_backward_kernel, grid=(seqs, PAIRS), in_specs=[full,...  52.3 us
    pallas_call x1, Pallas kernels, mlp(): pl.pallas_call(mlp_kernel, grid=(tokens // tile,), in_specs=[tiled, whole...  46.9 us
    pallas_call x1, Pallas kernels, attn_forward(): pl.pallas_call(attn_forward_kernel, grid=(seqs, PAIRS), in_specs=[pl.Bloc...  40.3 us
    pallas_call x1, Pallas kernels, gather_weights(): pl.pallas_call(gather_kernel, in_specs=[pl.BlockSpec(memory_space=pltpu.V...  23.2 us
    pallas_call x1, Pallas kernels, finish(): pl.pallas_call(functools.partial(finish_kernel, 1.0 / sequences), grid=(4...  9.25 us

profile of v2, /device:TPU:0, one launch (start us, length us, event | category | flops | bytes accessed | tf_op | source)
XLA Modules:
  0.0 250.1 jit_solution(220343767614681526)
XLA Ops:
  0.7 2.0 select_convert_fusion
  2.7 23.2 %gather_weights.1.w_ref = bf16[4,3584,128]{2,1,0:T(8,128)(2,1)} custom-call(f32[3467,128]{1,0:T(8,128)} %bitcast.18), custom_call_target="tpu_custom_call" | custom-call | tf_op jit(solution)/shard_map/gather_weights/pallas_call | solution.py:672
  25.9 1.3 slice_bitcast_fusion.1.vec_ref
  27.3 40.3 %attn_forward.1 = (bf16[2,1024,384]{2,1,0:T(8,128)(2,1)}, bf16[2,3,512,2560]{3,2,1,0:T(8,128)(2,1)}, bf16[2,3,1024,128]{3,2,1,0:T(8,128)(2,1)}, bf16[2,3,1024,12...) custom-call(bf16[2,1024,384]{2,1,0:T(8,128)(2,1)} %x_ref.3, ...), custom_call_target="tpu_custom_call" | custom-call | tf_op jit(solution)/shard_map/attn_forward/pallas_call | solution.py:194
  67.6 46.9 %mlp.1 = (bf16[2048,384]{1,0:T(8,128)(2,1)}, bf16[2048,384]{1,0:T(8,128)(2,1)}, f32[2048,384]{1,0:T(8,128)}, bf16[4,3584,128]{2,1,0:T(8,128)(2,1)}, f32[80,128]{1,0:T(8,128)}) custom-call(bf16[2048,384]{1,0:T(8,128)(2,1)} %bitcast.21, bf16[2048,384]{1,0:T(8,128)(2,1)} %bitcast.26, bf16[2048,384]{1,0:T(8,128)(2,1)} %bitcast.29, ...), custom_call_target="tpu_custom_call" | custom-call | tf_op jit(solution)/shard_map/mlp/pallas_call | solution.py:336
  114.5 52.3 %attn_backward.1 = (bf16[2,1024,384]{2,1,0:T(8,128)(2,1)}, bf16[4,3584,128]{2,1,0:T(8,128)(2,1)}) custom-call(bf16[2,1024,384]{2,1,0:T(8,128)(2,1)} %x_ref.3, f32[2,1024,384]{2,1,0:T(8,128)} %bitcast.27, bf16[2,1024,384]{2,1,0:T(8,128)(2,1)} %bitcast.28, bf16[2,1024,384]{2,1,0:T(8,128)(2,1)} %get-tuple-element.34.att_ref, ...), custom_call_target="tpu_custom_call", output_to_operand_aliasing={{1}: (16, {})} | custom-call | tf_op jit(solution)/shard_map/attn_backward/pallas_call | solution.py:520
  166.7 72.7 %reduce_gradients.1 = (bf16[3584,128]{1,0:T(8,128)(2,1)}, bf16[4,3584,128]{2,1,0:T(8,128)(2,1)}, f32[64,128]{1,0:T(8,128)}) custom-call(bf16[4,3584,128]{2,1,0:T(8,128)(2,1)} %get-tuple-element.51.g_ref, f32[3467,128]{1,0:T(8,128)} %bitcast.19, f32[3467,128]{1,0:T(8,128)} %bitcast.22, f32[3467,128]{1,0:T(8,128)} %bitcast.24), custom_call_target="tpu_custom_call" | custom-call | tf_op jit(solution)/shard_map/reduce_gradients/pallas_call | solution.py:826
  239.5 1.4 slice_bitcast_fusion
  240.8 9.2 %finish.1 = (f32[3467,128]{1,0:T(8,128)}, f32[3467,128]{1,0:T(8,128)}, f32[3467,128]{1,0:T(8,128)}, f32[3467,128]{1,0:T(8,128)}, bf16[13868,128]{1,0:T(8,128)(2,1)}) custom-call(bf16[3584,128]{1,0:T(8,128)(2,1)} %get-tuple-element.52.sum_ref, f32[3467,128]{1,0:T(8,128)} %bitcast.20, f32[3467,128]{1,0:T(8,128)} %bitcast.23, f32[3467,128]{1,0:T(8,128)} %bitcast.25, ...), custom_call_target="tpu_custom_call" | custom-call | tf_op jit(solution)/shard_map/finish/pallas_call | solution.py:883
  (2 shorter events, 0.0 us)
